TPU v7x, 32 devices: a whole 2x2x4 slice. The times are simulated.
32 devices in a mesh: slides: 2 (over y), seq: 16 (over z, x, core), mp: 1.
Axes of the slice: x: 2, y: 2, z: 4, core: 2. Of those that a mesh axis runs over, the one named last changes fastest.
Arguments:
- tokens: bfloat16 [32768, 768], P(('slides', 'seq', 'mp')), parts along dimension 0, may hold values from -6 to 6
- attn_gain: float32 [768], replicated, may hold values from 0.25 to 1.75
- query_first: bfloat16 [768, 768], P(None, 'mp'), may hold values from -4 to 4
- key_first: bfloat16 [768, 768], P(None, 'mp'), may hold values from -4 to 4
- segment_value: bfloat16 [768, 768], P(None, 'mp'), may hold values from -0.21875 to 0.21875
- output_first: bfloat16 [768, 768], P('mp'), may hold values from -0.875 to 0.875
- mlp_gain: float32 [768], replicated, may hold values from 0.25 to 1.75
- up_weight: bfloat16 [768, 3072], P(None, 'mp'), may hold values from -0.21875 to 0.21875
- down_weight: bfloat16 [3072, 768], P('mp'), may hold values from -0.109375 to 0.109375
- second_gain: float32 [768], replicated, may hold values from 0.25 to 1.75
- query_second: bfloat16 [768, 768], P(None, 'mp'), may hold values from -4 to 4
- key_second: bfloat16 [768, 768], P(None, 'mp'), may hold values from -4 to 4
- value_second: bfloat16 [768, 768], P(None, 'mp'), may hold values from -0.21875 to 0.21875
- output_second: bfloat16 [768, 768], P('mp'), may hold values from -0.875 to 0.875
- segment_offset: int32 [16], P('mp'), may hold values from 0 to 63
- global_offset: int32 [16], P('mp'), may hold values from 0 to 63
Outputs:
- encoded: bfloat16 [32768, 768], P(('slides', 'seq', 'mp')), parts along dimension 0
There are 2 independent parts, one for each index of `slides`. A program takes and returns all parts, laid end to end along the dimension named above; an argument that names none is the same for every part. Nothing has to cross between parts.
All inputs are finite; a program needn't handle non-finite values.
Results may differ from a plain program's by a relative error of at most 0.03.
The roundings to bfloat16 on the way count: a program that leaves them out, or rounds other values in their place, can miss the bound.
Values may be sent and summed in bfloat16 or wider, within the bound.
No kernel may reach another device: no remote copies, remote signals or barrier semaphores. Data moves between devices by JAX's collectives and lax.ppermute only.
A program may use at most 128 MiB of HBM per device.

v0:
```python
import functools
import math

import jax
import jax.numpy as jnp
from jax import lax
from jax.experimental import pallas as pl
from jax.experimental.pallas import tpu as pltpu
from jax.sharding import PartitionSpec as P

KEYS = 256
SEG_MAX = 16
ROWS = 256
LOG2E = 1.4426950408889634
BF16 = jnp.bfloat16
F32 = jnp.float32
VMEM_LIMIT = 22 * 1024 * 1024


def swapped(x, axis, apart):
    return lax.ppermute(x, axis, [(i, i ^ 1 << apart) for i in range(lax.axis_size(axis))])


def norm_rows(values, gain):
    center = values - jnp.mean(values, axis=-1, keepdims=True)
    spread = jnp.mean(center * center, axis=-1, keepdims=True)
    return (center * lax.rsqrt(spread + 1e-05) * gain).astype(jnp.bfloat16)


def pick_keys(hidden, offsets, stride, key_weight, value_weight):
    token_count, width = hidden.shape
    head_count = offsets.shape[0]
    head_size = key_weight.shape[1] // head_count
    grouped_rows = hidden.reshape(token_count // stride, stride, width)
    dilation_selector = (
        lax.broadcasted_iota(jnp.int32, (stride, head_count), 0) == offsets[None, :]
    ).astype(jnp.bfloat16)
    chosen = jnp.einsum(
        "nof,oj->njf", grouped_rows, dilation_selector, preferred_element_type=jnp.float32
    ).astype(jnp.bfloat16)
    key_heads = jnp.einsum(
        "xkr,rkf->xkf",
        chosen,
        key_weight.reshape(width, head_count, head_size),
        preferred_element_type=jnp.float32,
    ).astype(jnp.bfloat16)
    value_heads = jnp.einsum(
        "xkr,rkf->xkf",
        chosen,
        value_weight.reshape(width, head_count, head_size),
        preferred_element_type=jnp.float32,
    ).astype(jnp.bfloat16)
    picked = token_count // stride
    return jnp.stack(
        [
            key_heads.reshape(picked, head_count * head_size),
            value_heads.reshape(picked, head_count * head_size),
        ]
    )


def attend_local(query, keyval, head_count):
    token_count, width = query.shape
    head_size = width // head_count
    query_heads = query.reshape(token_count, head_count, head_size)
    key_heads = keyval[0].reshape(-1, head_count, head_size)
    value_heads = keyval[1].reshape(-1, head_count, head_size)
    scores = jnp.einsum(
        "thd,khd->htk", query_heads, key_heads, preferred_element_type=jnp.float32
    ) * head_size ** (-0.5)
    highest = jnp.max(scores, axis=-1, keepdims=True)
    weights = jnp.exp(scores - highest)
    weights = (weights / jnp.sum(weights, axis=-1, keepdims=True)).astype(jnp.bfloat16)
    mixed = jnp.einsum(
        "htk,khd->thd", weights, value_heads, preferred_element_type=jnp.float32
    ).astype(jnp.bfloat16)
    return mixed.reshape(token_count, width)


def merge_branch_pair(mine, other, level, token_position):
    lower = token_position >> level & 1 == 0
    return jnp.where(
        lower, jnp.concatenate((mine, other), axis=1), jnp.concatenate((other, mine), axis=1)
    )


def spread_segment(keyval, seg_span, token_position):
    for level in range(seg_span.bit_length() - 1):
        partner = swapped(keyval, "seq", level)
        keyval = merge_branch_pair(keyval, partner, level, token_position)
    return keyval


def spread_global(keyval_two):
    keyval_two = lax.all_gather(keyval_two, "seq", axis=1, tiled=True)
    return keyval_two


def combine(partial_value, residual_full, need_full):
    row_count = residual_full.shape[0] // lax.axis_size("mp")
    row_start = lax.axis_index("mp") * row_count
    share = lax.psum_scatter(partial_value, "mp", scatter_dimension=0, tiled=True)
    own_rows = lax.dynamic_slice_in_dim(residual_full, row_start, row_count, 0)
    own_rows = (own_rows.astype(jnp.float32) + share).astype(jnp.bfloat16)
    full_rows = lax.all_gather(own_rows, "mp", axis=0, tiled=True) if need_full else own_rows
    return (own_rows, full_rows)


def split_body(
    tokens,
    attn_gain,
    query_first,
    key_first,
    segment_value,
    output_first,
    mlp_gain,
    up_weight,
    down_weight,
    second_gain,
    query_second,
    key_second,
    value_second,
    output_second,
    segment_offset,
    global_offset,
):
    seq_count = lax.axis_size("seq")
    token_position = lax.axis_index("seq")
    seg_span = min(SEG_MAX, seq_count)
    head_count = segment_offset.shape[0]
    full_rows = lax.all_gather(tokens, "mp", axis=0, tiled=True)
    token_count = full_rows.shape[0]
    hidden = norm_rows(full_rows.astype(jnp.float32), attn_gain)
    query = jnp.dot(hidden, query_first, preferred_element_type=jnp.float32).astype(jnp.bfloat16)
    seg_stride = token_count // (KEYS // seg_span)
    keyval = pick_keys(hidden, segment_offset, seg_stride, key_first, segment_value)
    keyval = spread_segment(keyval, seg_span, token_position)
    mixed = attend_local(query, keyval, head_count)
    partial_value = jnp.dot(mixed, output_first, preferred_element_type=jnp.float32)
    own_rows, first_rows = combine(partial_value, full_rows, True)
    normed = norm_rows(first_rows.astype(jnp.float32), mlp_gain)
    inner = jax.nn.gelu(
        jnp.dot(normed, up_weight, preferred_element_type=jnp.float32), approximate=True
    ).astype(jnp.bfloat16)
    partial_value = jnp.dot(inner, down_weight, preferred_element_type=jnp.float32)
    own_rows, second_rows = combine(partial_value, first_rows, True)
    hidden_two = norm_rows(second_rows.astype(jnp.float32), second_gain)
    query_two = jnp.dot(hidden_two, query_second, preferred_element_type=jnp.float32).astype(
        jnp.bfloat16
    )
    glob_stride = token_count // (KEYS // seq_count)
    keyval_two = pick_keys(hidden_two, global_offset, glob_stride, key_second, value_second)
    keyval_two = spread_global(keyval_two)
    mixed_two = attend_local(query_two, keyval_two, head_count)
    partial_value = jnp.dot(mixed_two, output_second, preferred_element_type=jnp.float32)
    own_rows, unused_rows = combine(partial_value, second_rows, False)
    return own_rows


def one_hot(condition):
    return jnp.where(condition, 1.0, 0.0).astype(BF16)


def dot(left, right):
    return jnp.dot(left, right, preferred_element_type=F32)


def pieces(count, size):
    size = size if count % size == 0 else count
    return [slice(start, start + size) for start in range(0, count, size)]


def norm_into(out, start, source, gain, count):
    for span in pieces(count, 64):
        out[start + span.start : start + span.stop, :] = norm_rows(
            source[span, :].astype(F32), gain
        )


def bring(source, target, sem):
    copy = pltpu.make_async_copy(source, target, sem)
    copy.start()
    return copy


def pick_matrix(offsets, heads, groups, stride):
    count = groups * stride
    place = lax.broadcasted_iota(jnp.int32, (groups, count), 1)
    place = place - lax.broadcasted_iota(jnp.int32, (groups, count), 0) * stride
    return jnp.concatenate([one_hot(place == offsets[h]) for h in range(heads)], axis=0)


def project_keys(chosen, heads, weights, keyval_ref):
    rows, width = chosen.shape
    groups, head_size = rows // heads, width // heads
    for slot, weight in enumerate(weights):
        held = weight()
        for span in pieces(width, 256):
            first, last = span.start // head_size, (span.stop - 1) // head_size + 1
            wide = dot(chosen[first * groups : last * groups], held[:, span])
            column = lax.broadcasted_iota(jnp.int32, (groups, span.stop - span.start), 1)
            total = wide[:groups]
            for h in range(first + 1, last):
                row = (h - first) * groups
                own = column >= h * head_size - span.start
                total = jnp.where(own, wide[row : row + groups], total)
            total = total.astype(BF16)
            for copy in range(keyval_ref.shape[0]):
                keyval_ref[copy, slot, :, span] = total


def ranks(offsets, chunk, stride, share, axis):
    heads = offsets.shape[0]

    def places(way):
        shape = (1, chunk) if way else (chunk, 1)
        place = lax.broadcasted_iota(jnp.int32, shape, way)
        inside = lax.rem(place, stride)
        taken = inside == offsets[0]
        for h in range(1, heads):
            taken = taken | (inside == offsets[h])
        return place, inside, jnp.where(taken, inside, inside + stride)

    place, inside, order = places(axis)
    other_place, _, other_order = places(1 - axis)
    ahead = (other_order < order) & (lax.div(other_place, stride) == lax.div(place, stride))
    rank = jnp.sum(jnp.where(ahead, 1, 0), axis=1 - axis, keepdims=True)
    group = lax.div(place, stride)
    return jnp.where(
        rank < heads, group * heads + rank, share + group * (stride - heads) + rank - heads
    )


def slots_of(offsets, heads):
    values = [offsets[h] for h in range(heads)]
    fresh = []
    for h in range(heads):
        seen = jnp.int32(1)
        for earlier in values[:h]:
            seen = jnp.where(earlier == values[h], 0, seen)
        fresh.append(seen)
    slots = []
    for h in range(heads):
        slot = jnp.int32(0)
        for other in range(heads):
            slot = slot + jnp.where(values[other] < values[h], fresh[other], 0)
        slots.append(slot)
    return slots


def first_keys_kernel(
    offsets, tokens, gain, key_weight, value_weight, keyval, rows, wide, picks, scale, sems, *, stride
):
    copies = [
        bring(offsets, picks, sems.at[0]),
        bring(tokens, rows, sems.at[1]),
        bring(gain, scale, sems.at[2]),
        bring(key_weight, wide.at[0], sems.at[3]),
        bring(value_weight, wide.at[1], sems.at[4]),
    ]
    heads = offsets.shape[0]
    copies[0].wait()
    chooser = pick_matrix(picks, heads, rows.shape[0] // stride, stride)
    copies[1].wait()
    copies[2].wait()
    chosen = norm_rows(dot(chooser, rows[...]), scale[...])

    def weight(slot):
        copies[slot + 3].wait()
        return wide[slot]

    project_keys(
        chosen, heads, [functools.partial(weight, slot) for slot in range(2)], keyval
    )


def order_kernel(
    offsets,
    tokens,
    gain,
    moved_rows,
    normed,
    chooser,
    back,
    rows,
    picks,
    scale,
    sems,
    *,
    stride,
    chunk,
):
    copies = [
        bring(offsets, picks, sems.at[0]),
        bring(tokens, rows, sems.at[1]),
        bring(gain, scale, sems.at[2]),
    ]
    count = tokens.shape[0]
    share = chunk // stride * offsets.shape[0]
    rest = chunk - share
    picked = count // chunk * share
    copies[0].wait()
    mover = one_hot(
        lax.broadcasted_iota(jnp.int32, (chunk, chunk), 0)
        == ranks(picks, chunk, stride, share, 1)
    )
    heads = offsets.shape[0]
    chooser[...] = pick_matrix(slots_of(picks, heads), heads, picked // heads, heads)
    back[...] = one_hot(
        lax.broadcasted_iota(jnp.int32, (chunk, chunk), 1)
        == ranks(picks, chunk, stride, share, 0)
    )
    copies[1].wait()
    copies[2].wait()
    for c in range(count // chunk):
        moved = dot(mover, rows[c * chunk : (c + 1) * chunk, :]).astype(BF16)
        moved_rows[c * share : (c + 1) * share, :] = moved[:share]
        moved_rows[picked + c * rest : picked + (c + 1) * rest, :] = moved[share:]
    norm_into(normed, 0, moved_rows, scale[...], count)


def scaled_query(normed, weight, outs, heads, peaks):
    width = normed.shape[1]
    factor = (width // heads) ** (-0.5) * LOG2E
    peak = None
    for out, row in outs:
        for span in pieces(out.shape[0], 512 if out.shape[0] % 512 == 0 else 256):
            query = dot(normed[row + span.start : row + span.stop, :], weight[...]) * factor
            out[span, :] = query.astype(BF16)
            for part in pieces(query.shape[0], 64):
                square = query[part] * query[part]
                peak = square if peak is None else jnp.maximum(peak, square)
    peaks[...] = summed_peaks(peak.astype(BF16), heads)


def first_query_kernel(normed, weight, picked, rest, peaks, sems, *, heads):
    del sems
    scaled_query(normed, weight, [(picked, 0), (rest, picked.shape[0])], heads, peaks)


def head_windows(head_size, width):
    period = min(width, math.lcm(head_size, 128))
    windows = []
    for h in range(period // head_size):
        start = h * head_size // 128 * 128
        stop = min(period, -(-(h + 1) * head_size // 128) * 128)
        windows.append((start, stop - start))
    return period, windows


def summed_peaks(peak, heads):
    width = peak.shape[1]
    column = lax.broadcasted_iota(jnp.int32, (width, 128), 0)
    head = lax.broadcasted_iota(jnp.int32, (width, 128), 1)
    low = head * (width // heads)
    sums = one_hot((column >= low) & (column < low + width // heads))
    return jnp.max(dot(peak, sums), axis=0, keepdims=True)


def load_keys(keyval, turned):
    keys = jnp.concatenate([keyval[i, 0] for i in range(keyval.shape[0])], axis=0)
    turned[...] = keys.T
    return keys * keys


def small_scores(query_peaks, key_peaks):
    return jnp.max(query_peaks[...] * key_peaks[...]) < 9000.0


def reciprocal(x):
    guess = pl.reciprocal(x, approx=True)
    return guess * (2.0 - x * guess)


def padded_keys(turned, base, head, head_size, start, size):
    low = base + head * head_size
    rows = pl.ds(low if isinstance(low, int) else pl.multiple_of(low, 16), head_size)
    own = jnp.concatenate([part[rows, :] for part in turned], axis=1)
    low = head * head_size - start
    parts = [own]
    if low:
        parts.insert(0, jnp.zeros((low, own.shape[1]), BF16))
    if low + head_size < size:
        parts.append(jnp.zeros((size - low - head_size, own.shape[1]), BF16))
    return jnp.concatenate(parts, axis=0)


def score_pair(query, span, base, head, head_size, windows, turned):
    start = windows[head][0]
    size = windows[head + 1][0] + windows[head + 1][1] - start
    keys = [padded_keys([turned], base, head + i, head_size, start, size) for i in range(2)]
    return dot(query[span, pl.ds(base + start, size)], jnp.concatenate(keys, axis=1))


def near_weights_kernel(
    picked, rest, keyval, picked_early, rest_early, turned, peaks, scores_ref, sems, *, heads
):
    del sems
    peaks[...] = summed_peaks(load_keys(keyval, turned), heads)
    width = picked.shape[1]
    head_size = width // heads
    key_count = turned.shape[1]
    period, windows = head_windows(head_size, width)
    jobs = [
        (query, early, head)
        for query, early in ((picked, picked_early), (rest, rest_early))
        for head in range(0, len(windows), 2)
    ]

    @pl.loop(0, width // period)
    def _(turn):
        base = pl.multiple_of(turn * period, 128)

        def score(i):
            query, _, head = jobs[i]
            rows = query.shape[0]
            scores_ref[i % 2, :rows] = score_pair(
                query, slice(0, rows), base, head, head_size, windows, turned
            )

        score(0)
        for i, (query, early, head) in enumerate(jobs):
            if i + 1 < len(jobs):
                score(i + 1)
            for part in pieces(query.shape[0], 64):
                weights = jnp.exp2(scores_ref[i % 2, part, :]).astype(BF16)
                for j in range(2):
                    early[turn * len(windows) + head + j, part, :] = weights[
                        :, j * key_count : (j + 1) * key_count
                    ]


def attend_rows(
    query, first_row, rows, heads, turned, keyvals, mixed_ref, mixed_row, work, plain, early=None
):
    scores_ref, weights_ref = work
    width = query.shape[1]
    key_count = sum(part.shape[1] for part in turned)
    head_size = width // heads
    period, windows = head_windows(head_size, width)
    span = pl.ds(first_row, rows)
    out_span = pl.ds(mixed_row, rows)
    lane = lax.broadcasted_iota(jnp.int32, (1, 128), 1)
    step = 2 if early is not None else 1

    def take_turn(turn):
        base = turn * period if plain else pl.multiple_of(turn * period, 128)
        sums = {}

        def score(i):
            if early is not None:
                scores = score_pair(query, span, base, 2 * i, head_size, windows, turned[1])
            else:
                start, size = windows[i]
                scores = dot(
                    query[span, pl.ds(base + start, size)],
                    padded_keys(turned, base, i, head_size, start, size),
                )
            scores_ref[i % 2, :rows] = scores

        def weigh(h):
            for part in pieces(rows, 64):
                scores = scores_ref[h % 2, part, :]
                if not plain:
                    scores = scores - jnp.max(scores, axis=1, keepdims=True)
                weights_ref[h % 2, part, :] = jnp.exp2(scores).astype(BF16)

        def mix(h):
            start, size = windows[h]
            low = h * head_size - start
            values = jnp.concatenate(
                [
                    x[i, 1, :, pl.ds(base + start, size)]
                    for x in keyvals
                    for i in range(x.shape[0])
                ],
                axis=0,
            )
            column = lax.broadcasted_iota(jnp.int32, (key_count, size), 1)
            own = (column >= low) & (column < low + head_size)
            values = jnp.where(own, values, jnp.ones((), BF16))
            if early is not None:
                half = key_count // 2
                far = weights_ref[h // 2 % 2, :rows, h % 2 * half : (h % 2 + 1) * half]
                near = early[turn * len(windows) + h, span, :]
                weights = jnp.concatenate([near, far], axis=1)
            else:
                weights = weights_ref[h % 2, :rows]
            mixed = dot(weights, values)
            for offset in range(0, size, 128):
                own = mixed[:, offset : offset + 128]
                own = own * reciprocal(pltpu.roll(own, 64, 1))
                at = start + offset
                if at in sums:
                    own = jnp.where(lane >= h * head_size - at, own, sums[at])
                sums[at] = own
                if (h + 1) * head_size >= at + 128:
                    mixed_ref[out_span, pl.ds(base + at, 128)] = sums.pop(at).astype(BF16)

        count = len(windows) // step
        score(0)
        for i in range(count):
            if i:
                for h in range((i - 1) * step, i * step):
                    mix(h)
            if i + 1 < count:
                score(i + 1)
            weigh(i)
        for h in range((count - 1) * step, count * step):
            mix(h)

    if plain:
        for turn in range(width // period):
            take_turn(turn)
    else:
        pl.loop(0, width // period)(take_turn)


def attend(query, rows, heads, turned, keyvals, mixed_ref, work, small, early=None):
    size = math.gcd(rows, ROWS)

    @pl.when(small)
    def _():
        attend_rows(query, 0, rows, heads, turned, keyvals, mixed_ref, 0, work, True, early)

    @pl.when(jnp.logical_not(small))
    def _():
        @pl.loop(0, rows // size)
        def _(step):
            row = pl.multiple_of(step * size, size)
            attend_rows(
                query,
                row,
                size,
                heads,
                turned,
                keyvals,
                mixed_ref,
                row,
                work,
                False,
            )


def gelu(x):
    half = 0.5 * x
    return half + half * jnp.tanh(x * (0.7978845608028654 + 0.035677408136300125 * (x * x)))


def widen(normed, up_weight, low, wide_ref, inner):
    rows = normed.shape[0]
    spans = pieces(inner.shape[1], wide_ref.shape[2])

    def product(i):
        columns = slice(low + spans[i].start, low + spans[i].stop)
        wide_ref[i % 2] = dot(normed[...], up_weight[:, columns])

    product(0)
    for i, span in enumerate(spans):
        if i + 1 < len(spans):
            product(i + 1)
        for part in pieces(rows, 32):
            inner[part, span] = gelu(wide_ref[i % 2, part, :]).astype(BF16)


def feed_forward(normed, up_weight, down_weight, total, wide_ref, inner):
    rows = normed.shape[0]
    spans = pieces(up_weight.shape[1], wide_ref.shape[2])

    def product(i):
        wide_ref[i % 2] = dot(normed[...], up_weight[:, spans[i]])

    product(0)
    for i, span in enumerate(spans):
        if i + 1 < len(spans):
            product(i + 1)
        for part in pieces(rows, 32):
            inner[i % 2, part, :] = gelu(wide_ref[i % 2, part, :]).astype(BF16)
        total[...] += dot(inner[i % 2], down_weight[span, :])


def narrow(inners, down_weight, first, second, size):
    for span in pieces(second.shape[1], size):
        total = first[:, span].astype(F32)
        low = 0
        for inner in inners:
            high = low + inner.shape[1]
            total = total + dot(inner[...], down_weight[low:high, span])
            low = high
        second[:, span] = total.astype(BF16)


def add_heads(tokens, first_row, mixed, out_weight, gain, first, normed):
    before = None
    for span in pieces(mixed.shape[0], 256):
        total = dot(mixed[span, :], out_weight[...])
        rows = tokens[first_row + span.start : first_row + span.stop, :]
        first[span, :] = (rows.astype(F32) + total).astype(BF16)
        if before is not None:
            norm_into(normed, before.start, first.at[before], gain, before.stop - before.start)
        before = span
    norm_into(normed, before.start, first.at[before], gain, before.stop - before.start)


def picked_kernel(
    chooser,
    tokens,
    query,
    query_peaks,
    early,
    keyval,
    keyval_far,
    turned_near,
    peaks_near,
    out_weight,
    mlp_gain,
    up_weight,
    down_weight,
    gain,
    key_weight,
    value_weight,
    second,
    normed,
    keyval_two,
    turned,
    peaks,
    held,
    mixed,
    scores,
    weights,
    first,
    wide,
    inner,
    total,
    sems,
    *,
    heads,
):
    copies = [
        bring(x, held.at[i], sems.at[i]) for i, x in enumerate((key_weight, value_weight))
    ]
    rows = second.shape[0]
    keyvals = (keyval, keyval_far)
    squares = load_keys(keyval_far, turned)
    peaks[...] = jnp.maximum(peaks_near[...], summed_peaks(squares, heads))
    small = small_scores(query_peaks, peaks)
    attend(
        query,
        rows,
        heads,
        (turned_near, turned),
        keyvals,
        mixed,
        (scores, weights),
        small,
        early,
    )
    add_heads(tokens, 0, mixed, out_weight, mlp_gain[...], first, normed)
    total[...] = first[...].astype(F32)
    feed_forward(normed, up_weight, down_weight, total, wide, inner)
    second[...] = total[...].astype(BF16)
    norm_into(normed, 0, second, gain[...], rows)
    chosen = dot(chooser[...], normed[...]).astype(BF16)

    def weight(slot):
        copies[slot].wait()
        return held[slot]

    project_keys(
        chosen, heads, [functools.partial(weight, slot) for slot in range(2)], keyval_two
    )


def rest_attention_kernel(
    query,
    query_peaks,
    early,
    keyval,
    keyval_far,
    turned_near,
    turned,
    peaks,
    mixed,
    scores,
    weights,
    sems,
    *,
    heads,
):
    del sems
    attend(
        query,
        mixed.shape[0],
        heads,
        (turned_near, turned),
        (keyval, keyval_far),
        mixed,
        (scores, weights),
        small_scores(query_peaks, peaks),
        early,
    )


def rest_up_kernel(
    tokens, mixed, out_weight, gain, up_weight, first, normed, inner, wide, sems
):
    del sems
    add_heads(
        tokens, tokens.shape[0] - mixed.shape[0], mixed, out_weight, gain[...], first, normed
    )
    widen(normed, up_weight, 0, wide, inner)


def rest_down_kernel(
    first, normed, inner, up_weight, down_weight, second, wide, inner_more, sems
):
    del sems
    widen(normed, up_weight, inner.shape[1], wide, inner_more)
    narrow([inner, inner_more], down_weight, first, second, 256)


def picked_query_kernel(normed, weight, query, peaks, sems, *, heads):
    del sems
    scaled_query(normed, weight, [(query, 0)], heads, peaks)


def rest_query_kernel(
    picked, picked_peaks, rows, gain, weight, query, peaks, normed, sems, *, heads
):
    del sems
    start = picked.shape[0]
    query[:start, :] = picked[...]
    norm_into(normed, 0, rows, gain[...], rows.shape[0])
    out = query.at[pl.ds(start, rows.shape[0])]
    scaled_query(normed, weight, [(out, 0)], heads, peaks)
    peaks[...] = jnp.maximum(peaks[...], picked_peaks[...])


def second_kernel(*refs, heads, parts):
    back, *rows = refs[: 1 + parts]
    query, query_peaks, keyval, keyval_far, out_weight, encoded = refs[1 + parts : 7 + parts]
    turned_near, turned, held, mixed = refs[7 + parts : 11 + parts]
    result, ready, scores, weights, sems = refs[11 + parts :]
    copy = bring(out_weight, held.at[0], sems.at[0])
    keyvals = (keyval, keyval_far)
    squares = jnp.maximum(load_keys(keyval, turned_near), load_keys(keyval_far, turned))
    count = query.shape[0]
    small = small_scores(query_peaks, summed_peaks(squares, heads))
    attend(
        query, count, heads, (turned_near, turned), keyvals, mixed, (scores, weights), small
    )
    chunk = back.shape[0]
    share = rows[0].shape[0] * chunk // count
    rest_share = chunk - share
    copy.wait()
    start = 0
    for part in rows:
        span = slice(start, start + part.shape[0])
        total = part[...].astype(F32) + dot(mixed[span, :], held[0])
        result[span, :] = total.astype(BF16)
        start += part.shape[0]
    start = count // chunk * share
    copies = []
    for c in range(count // chunk):
        far = start + c * rest_share
        blend = jnp.concatenate(
            [result[c * share : (c + 1) * share, :], result[far : far + rest_share, :]], axis=0
        )
        span = pl.ds(c * chunk, chunk)
        ready[span, :] = dot(back[...], blend).astype(BF16)
        copies.append(bring(ready.at[span], encoded.at[span], sems.at[1 + c]))
    for copy in copies:
        copy.wait()


def relaying(kernel, ins, outs, *refs):
    end = ins + 1 + outs
    refs[end][...] = refs[ins][...]
    kernel(*refs[:ins], *refs[ins + 1 : end], *refs[end + 1 :])


def local_call(kernel, outs, inputs, scratch, scalars=0, far=(), relay=None, out_near=True, copies=1, flops=0, name=None):
    outs, inputs = list(outs), list(inputs)
    if relay is not None:
        kernel = functools.partial(relaying, kernel, len(inputs), len(outs))
        inputs.append(relay)
        outs.append(pltpu.VMEM(relay.shape, relay.dtype))
    specs, placed = [], []
    for i, x in enumerate(inputs):
        if i < scalars:
            specs.append(pl.BlockSpec(memory_space=pltpu.SMEM))
        elif i in far:
            specs.append(pl.BlockSpec(memory_space=pltpu.HBM))
            x = pltpu.with_memory_space_constraint(x, pltpu.HBM)
        else:
            specs.append(pl.BlockSpec(memory_space=pltpu.VMEM))
            x = pltpu.with_memory_space_constraint(x, pltpu.VMEM)
        placed.append(x)
    return pl.pallas_call(
        kernel,
        out_shape=outs,
        in_specs=specs,
        out_specs=[
            pl.BlockSpec(memory_space=pltpu.VMEM if out_near else pltpu.HBM)
        ] * len(outs),
        scratch_shapes=list(scratch) + [pltpu.SemaphoreType.DMA((copies,))],
        compiler_params=pltpu.CompilerParams(vmem_limit_bytes=VMEM_LIMIT),
        cost_estimate=pl.CostEstimate(
            flops=int(flops),
            transcendentals=0,
            bytes_accessed=sum(inputs[i].size * inputs[i].dtype.itemsize for i in far),
        ),
        name=name,
    )(*placed)


def exchange(keyval, span, beside):
    size = lax.axis_size("seq")
    levels = span.bit_length() - 1
    even = list(range(levels - 1, 0, -1))
    orders = (even, even[-1:] + even[:-1])
    for step in range(levels - 1):
        pairs = [(i, i ^ 1 << orders[i % 2][step]) for i in range(size)]
        partner = lax.ppermute(keyval, "seq", pairs)
        keyval = jnp.concatenate([beside(step, keyval), partner], axis=0)
    far = swapped(keyval, "seq", 0)
    return beside(levels - 1, keyval), far


def whole_body(
    tokens,
    attn_gain,
    query_first,
    key_first,
    segment_value,
    output_first,
    mlp_gain,
    up_weight,
    down_weight,
    second_gain,
    query_second,
    key_second,
    value_second,
    output_second,
    segment_offset,
    global_offset,
):
    seq_count = lax.axis_size("seq")
    seg_span = min(SEG_MAX, seq_count)
    heads = segment_offset.shape[0]
    count, width = tokens.shape
    head_size = width // heads
    hidden = up_weight.shape[1]
    stride = count // (KEYS // seg_span)
    stride_two = count // (KEYS // seq_count)
    groups, groups_two = count // stride, count // stride_two
    chunk = max(ROWS, stride_two)
    picked_count = groups_two * heads
    rest_count = count - picked_count
    part = hidden // 4

    def near(*shape):
        return pltpu.VMEM(shape, BF16)

    def attention_work(rows):
        return [pltpu.VMEM((2, rows, KEYS), F32), near(2, rows, KEYS)]

    held_shapes = [near(width, KEYS // 2), pltpu.VMEM((1, 128), F32)]
    small_work = [pltpu.SMEM((heads,), jnp.int32), pltpu.VMEM((width,), F32)]

    (keyval,) = local_call(
        functools.partial(first_keys_kernel, stride=stride),
        [near(1, 2, groups, width)],
        (segment_offset, tokens, attn_gain, key_first, segment_value),
        [near(count, width), near(2, width, width)] + small_work,
        far=(0, 1, 2, 3, 4),
        copies=5,
        flops=2 * heads * groups * width * (count + 2 * width),
        name="first_keys",
    )
    made = {}

    def beside_first(level, held):
        if level == 0:
            made["rows"], made["normed"], made["chooser"], made["back"], held = local_call(
                functools.partial(order_kernel, stride=stride_two, chunk=chunk),
                [
                    near(count, width),
                    near(count, width),
                    near(picked_count, picked_count),
                    near(chunk, chunk),
                ],
                (global_offset, tokens, attn_gain),
                [near(count, width)] + small_work,
                far=(0, 1, 2),
                copies=3,
                relay=held,
                flops=2 * count * width * chunk,
                name="order",
            )
        if level == min(1, seg_span.bit_length() - 2):
            made["picked"], made["rest"], made["peaks"], held = local_call(
                functools.partial(first_query_kernel, heads=heads),
                [near(picked_count, width), near(rest_count, width), pltpu.VMEM((1, 128), F32)],
                (made["normed"], query_first),
                [],
                relay=held,
                flops=2 * count * width * width,
                name="first_query",
            )
        if level == seg_span.bit_length() - 2:
            made["picked_early"], made["rest_early"], made["turned"], made["key_peaks"] = local_call(
                functools.partial(near_weights_kernel, heads=heads),
                [near(heads, picked_count, KEYS // 2), near(heads, rest_count, KEYS // 2)]
                + held_shapes,
                (made["picked"], made["rest"], held),
                [pltpu.VMEM((2, rest_count, KEYS), F32)],
                flops=2 * 256 * KEYS // 2 * heads * count,
                name="near_weights",
            )
        return held

    keyval, keyval_far = exchange(keyval, seg_span, beside_first)
    rows = made["rows"]
    query_peaks, near_held = made["peaks"], (made["turned"], made["key_peaks"])
    row_flops = 2 * width * (2 * hidden + width) + 4 * 256 * KEYS * heads
    picked_second, picked_normed, keyval_two, turned, peaks = local_call(
        functools.partial(picked_kernel, heads=heads),
        [
            near(picked_count, width),
            near(picked_count, width),
            near(1, 2, groups_two, width),
        ]
        + held_shapes,
        (
            made["chooser"],
            rows,
            made["picked"],
            query_peaks,
            made["picked_early"],
            keyval,
            keyval_far,
            *near_held,
            output_first,
            mlp_gain,
            up_weight,
            down_weight,
            second_gain,
            key_second,
            value_second,
        ),
        [near(2, width, width), near(picked_count, width)]
        + attention_work(picked_count)
        + [near(picked_count, width), pltpu.VMEM((2, picked_count, part), F32)]
        + [near(2, picked_count, part), pltpu.VMEM((picked_count, width), F32)],
        far=(14, 15),
        copies=2,
        flops=row_flops * picked_count,
        name="layer_of_picked",
    )
    seconds = [picked_second]

    def rest_attention(held):
        made["mixed"], held = local_call(
            functools.partial(rest_attention_kernel, heads=heads),
            [near(rest_count, width)],
            (
                made["rest"],
                query_peaks,
                made["rest_early"],
                keyval,
                keyval_far,
                made["turned"],
                turned,
                peaks,
            ),
            attention_work(rest_count),
            relay=held,
            flops=4 * 256 * KEYS * heads * rest_count,
            name="rest_attention",
        )
        return held

    half = hidden // 4 * 3

    def rest_up(held):
        made["first"], made["normed"], made["inner"], held = local_call(
            rest_up_kernel,
            [near(rest_count, width), near(rest_count, width), near(rest_count, half)],
            (rows, made["mixed"], output_first, mlp_gain, up_weight),
            [pltpu.VMEM((2, rest_count, part), F32)],
            relay=held,
            flops=2 * width * (half + width) * rest_count,
            name="rest_up",
        )
        return held

    def rest_down(held):
        result, held = local_call(
            rest_down_kernel,
            [near(rest_count, width)],
            (made["first"], made["normed"], made["inner"], up_weight, down_weight),
            [pltpu.VMEM((1, rest_count, part), F32), near(rest_count, hidden - half)],
            relay=held,
            flops=2 * width * (2 * hidden - half) * rest_count,
            name="rest_down",
        )
        seconds.append(result)
        return held

    def picked_query(held):
        made["picked_two"], made["picked_peaks"], held = local_call(
            functools.partial(picked_query_kernel, heads=heads),
            [near(picked_count, width), pltpu.VMEM((1, 128), F32)],
            (picked_normed, query_second),
            [],
            relay=held,
            flops=2 * picked_count * width * width,
            name="picked_query",
        )
        return held

    def rest_query(held):
        made["query_two"], made["peaks_two"], held = local_call(
            functools.partial(rest_query_kernel, heads=heads),
            [near(count, width), pltpu.VMEM((1, 128), F32)],
            (made["picked_two"], made["picked_peaks"], seconds[1], second_gain, query_second),
            [near(rest_count, width)],
            relay=held,
            flops=2 * rest_count * width * width,
            name="rest_query",
        )
        return held

    tasks = [[rest_attention], [rest_up, picked_query], [rest_down], [rest_query]]
    levels = seq_count.bit_length() - 1

    def beside_second(level, held):
        for work in tasks[len(tasks) * level // levels : len(tasks) * (level + 1) // levels]:
            for task in work:
                held = task(held)
        return held

    keyval_two, keyval_two_far = exchange(keyval_two, seq_count, beside_second)
    (encoded,) = local_call(
        functools.partial(second_kernel, heads=heads, parts=len(seconds)),
        [jax.ShapeDtypeStruct((count, width), BF16)],
        (
            made["back"],
            *seconds,
            made["query_two"],
            made["peaks_two"],
            keyval_two,
            keyval_two_far,
            output_second,
        ),
        held_shapes[:1] * 2
        + [near(1, width, width)]
        + [near(count, width)] * 3
        + attention_work(count),
        far=(len(seconds) + 5,),
        out_near=False,
        copies=1 + count // chunk,
        flops=count * (2 * width * width + 4 * 256 * KEYS * heads),
        name="second_attention",
    )
    return encoded


def solution(mesh):
    placed = (
        P(("slides", "seq", "mp"), None),
        P(),
        P(None, "mp"),
        P(None, "mp"),
        P(None, "mp"),
        P("mp", None),
        P(),
        P(None, "mp"),
        P("mp", None),
        P(),
        P(None, "mp"),
        P(None, "mp"),
        P(None, "mp"),
        P("mp", None),
        P("mp"),
        P("mp"),
    )
    fits = mesh.shape["mp"] == 1 and mesh.shape["seq"] in (2, 4, 8, 16)
    return jax.shard_map(
        whole_body if fits else split_body,
        mesh=mesh,
        in_specs=placed,
        out_specs=P(("slides", "seq", "mp"), None),
        check_vma=False,
    )
```

profile of v0, /device:TPU:1, one launch (start us, length us, event | category | flops | bytes accessed | tf_op | source)
XLA Modules:
  0.0 83.8 jit_solution(6241749859320089352)
XLA Ops:
  0.0 3.2 %first_keys.1.refs_3_ = bf16[1,2,16,768]{3,2,1,0:T(8,128)(2,1)S(1)} custom-call(s32[16]{0:T(128)} %offsets.1, bf16[1024,768]{1,0:T(8,128)(2,1)} %refs_1_.3, f32[768]{0:T(1024)} %refs_2_.2, bf16[768,768]{1,0:T(8,128)(2,1)} %key_weight.2, bf16[768,768]{1,0:T(8,128)(2,1)} %value_weight.2), custom_call_target="tpu_custom_call" | custom-call | flops 1006632960 | bytes 3935296 | tf_op jit(solution)/shard_map/first_keys/pallas_call | solution.py:799
  3.3 2.1 %collective-permute-start = (bf16[1,2,16,768]{3,2,1,0:T(8,128)(2,1)S(1)}, bf16[1,2,16,768]{3,2,1,0:T(8,128)(2,1)S(1)}, u32[]{:S(2)}, u32[]{:S(2)}) collective-permute-start(bf16[1,2,16,768]{3,2,1,0:T(8,128)(2,1)S(1)} %first_keys.1.refs_3_), channel_id=1, source_target_pairs={{0,8},{1,3},{2,10},{3,1},{4,12},{5,7},{6,14},{7,5},{8,0},{9,11},{1... | collective-permute-start | bytes 147464 | tf_op jit(solution)/shard_map/ppermute | solution.py:824
  5.4 2.9 %order.1 = (bf16[1024,768]{1,0:T(8,128)(2,1)S(1)}, bf16[1024,768]{1,0:T(8,128)(2,1)S(1)}, bf16[256,256]{1,0:T(8,128)(2,1)S(1)}, bf16[256,256]{1,0:T(8,128)(2,1)S(1)}, bf16[1,2,16,768]{3,2,1,0:T(8,128)(2,1)S(1)}) custom-call(s32[16]{0:T(128)} %refs_0_.1, bf16[1024,768]{1,0:T(8,128)(2,1)} %refs_1_.3, f32[768]{0:T(1024)} %refs_2_.2, ...), custom_call_target="tpu_custom_call" | custom-call | flops 402653184 | bytes 1576000 | tf_op jit(solution)/shard_map/order/pallas_call | solution.py:799
  8.3 0.0 collective-permute-done
  8.3 2.4 %collective-permute-start.1 = (bf16[2,2,16,768]{3,2,1,0:T(8,128)(2,1)S(1)}, bf16[2,2,16,768]{3,2,1,0:T(8,128)(2,1)S(1)}, u32[]{:S(2)}, u32[]{:S(2)}) collective-permute-start(bf16[2,2,16,768]{3,2,1,0:T(8,128)(2,1)S(1)} %constant_dynamic-update-slice_fusion.refs_2_), channel_id=1, source_target_pairs={{0,4},{1,9},{2,6},{3,11},{4,0},{5,13},{6,2},{7,15},{8,12},{9,1},{1... | collective-permute-start | bytes 294920 | tf_op jit(solution)/shard_map/ppermute | solution.py:824
  10.7 0.0 copy-done.5
  10.7 1.6 %first_query.1 = (bf16[256,768]{1,0:T(8,128)(2,1)S(1)}, bf16[768,768]{1,0:T(8,128)(2,1)S(1)}, f32[1,128]{1,0:T(1,128)S(1)}, bf16[2,2,16,768]{3,2,1,0:T(8,128)(2,1)S(1)}) custom-call(bf16[1024,768]{1,0:T(8,128)(2,1)S(1)} %get-tuple-element.40.refs_0_, bf16[768,768]{1,0:T(8,128)(2,1)S(1)} %copy-done.5, ...), custom_call_target="tpu_custom_call" | custom-call | flops 1207959552 | tf_op jit(solution)/shard_map/first_query/pallas_call | solution.py:799
  12.3 0.4 collective-permute-done.1
  12.8 1.8 %collective-permute-start.2 = (bf16[4,2,16,768]{3,2,1,0:T(8,128)(2,1)S(1)}, bf16[4,2,16,768]{3,2,1,0:T(8,128)(2,1)S(1)}, u32[]{:S(2)}, u32[]{:S(2)}) collective-permute-start(bf16[4,2,16,768]{3,2,1,0:T(8,128)(2,1)S(1)} %pad_maximum_fusion), channel_id=1, source_target_pairs={{0,2},{1,5},{2,0},{3,7},{4,6},{5,1},{6,4},{7,3},{8,10},{9,13},{10,... | collective-permute-start | bytes 589832 | tf_op jit(solution)/shard_map/ppermute | solution.py:824
  14.6 3.0 %collective-permute-done.2 = bf16[4,2,16,768]{3,2,1,0:T(8,128)(2,1)S(1)} collective-permute-done((bf16[4,2,16,768]{3,2,1,0:T(8,128)(2,1)S(1)}, bf16[4,2,16,768]{3,2,1,0:T(8,128)(2,1)S(1)}, u32[]{:S(2)}, u32[]{:S(2)}) %collective-permute-start.2) | collective-permute-done | bytes 196640 | tf_op jit(solution)/shard_map/ppermute | solution.py:824
  17.7 3.2 %collective-permute-start.3 = (bf16[8,2,16,768]{3,2,1,0:T(8,128)(2,1)S(1)}, bf16[8,2,16,768]{3,2,1,0:T(8,128)(2,1)S(1)}, u32[]{:S(2)}, u32[]{:S(2)}) collective-permute-start(bf16[8,2,16,768]{3,2,1,0:T(8,128)(2,1)S(1)} %constant_dynamic-update-slice_fusion.2.keyval.refs_3_), channel_id=1, source_target_pairs={{0,1},{1,0},{2,3},{3,2},{4,5},{5,4},{6,7},{7,6},{8,9},{9,8},{10,11... | collective-permute-start | bytes 1179656 | tf_op jit(solution)/shard_map/ppermute | solution.py:21
  20.9 1.6 %near_weights.1 = (bf16[16,256,128]{2,1,0:T(8,128)(2,1)S(1)}, bf16[16,768,128]{2,1,0:T(8,128)(2,1)S(1)}, bf16[768,128]{1,0:T(8,128)(2,1)S(1)}, f32[1,128]{1,0:T(1,128)S(1)}) custom-call(bf16[256,768]{1,0:T(8,128)(2,1)S(1)} %get-tuple-element.42.picked.query, bf16[768,768]{1,0:T(8,128)(2,1)S(1)} %get-tuple-element.44.rest.refs_0_, ...), custom_call_target="tpu_custom_call" | custom-call | flops 1073741824 | tf_op jit(solution)/shard_map/near_weights/pallas_call | solution.py:799
  22.6 0.0 collective-permute-done.3.keyval_far.refs_4_
  22.6 0.0 slice-done
  22.6 0.0 slice-done.1
  22.6 0.0 copy-done.2
  22.6 0.0 copy-done
  22.6 9.7 %layer_of_picked.1 = (bf16[256,768]{1,0:T(8,128)(2,1)S(1)}, bf16[256,768]{1,0:T(8,128)(2,1)S(1)}, bf16[1,2,16,768]{3,2,1,0:T(8,128)(2,1)S(1)}, bf16[768,128]{1,0:T(8,128)(2,1)S(1)}, f32[1,128]{1,0:T(1,128)S(1)}) custom-call(bf16[256,256]{1,0:T(8,128)(2,1)S(1)} %get-tuple-element.38.chooser, bf16[1024,768]{1,0:T(8,128)(2,1)S(1)} %get-tuple-element.39.tokens.refs_0_, ...), custom_call_target="tpu_custom_call" | custom-call | flops 3791650816 | bytes 2359296 | tf_op jit(solution)/shard_map/layer_of_picked/pallas_call | solution.py:799
  32.4 1.3 %collective-permute-start.4 = (bf16[1,2,16,768]{3,2,1,0:T(8,128)(2,1)S(1)}, bf16[1,2,16,768]{3,2,1,0:T(8,128)(2,1)S(1)}, u32[]{:S(2)}, u32[]{:S(2)}) collective-permute-start(bf16[1,2,16,768]{3,2,1,0:T(8,128)(2,1)S(1)} %get-tuple-element.53.refs_8_), channel_id=1, source_target_pairs={{0,8},{1,3},{2,10},{3,1},{4,12},{5,7},{6,14},{7,5},{8,0},{9,11},{1... | collective-permute-start | bytes 147464 | tf_op jit(solution)/shard_map/ppermute | solution.py:824
  33.6 13.0 %rest_attention.1 = (bf16[768,768]{1,0:T(8,128)(2,1)S(1)}, bf16[1,2,16,768]{3,2,1,0:T(8,128)(2,1)S(1)}) custom-call(bf16[768,768]{1,0:T(8,128)(2,1)S(1)} %get-tuple-element.44.rest.refs_0_, f32[1,128]{1,0:T(1,128)S(1)} %get-tuple-element.43.query_peaks.refs_1_, bf16[16,768,128]{2,1,0:T(8,128)(2,1)S(1)} %get-tuple-element.50.refs_2_, ...), custom_call_target="tpu_custom_call" | custom-call | flops 3221225472 | tf_op jit(solution)/shard_map/rest_attention/pallas_call | solution.py:799
  46.7 0.0 collective-permute-done.4
  46.7 1.8 %collective-permute-start.5 = (bf16[2,2,16,768]{3,2,1,0:T(8,128)(2,1)S(1)}, bf16[2,2,16,768]{3,2,1,0:T(8,128)(2,1)S(1)}, u32[]{:S(2)}, u32[]{:S(2)}) collective-permute-start(bf16[2,2,16,768]{3,2,1,0:T(8,128)(2,1)S(1)} %constant_dynamic-update-slice_fusion.5.refs_5_), channel_id=1, source_target_pairs={{0,4},{1,9},{2,6},{3,11},{4,0},{5,13},{6,2},{7,15},{8,12},{9,1},{1... | collective-permute-start | bytes 294920 | tf_op jit(solution)/shard_map/ppermute | solution.py:824
  48.5 4.7 %rest_up.1 = (bf16[768,768]{1,0:T(8,128)(2,1)S(1)}, bf16[768,768]{1,0:T(8,128)(2,1)S(1)}, bf16[768,2304]{1,0:T(8,128)(2,1)S(1)}, bf16[2,2,16,768]{3,2,1,0:T(8,128)(2,1)S(1)}) custom-call(bf16[1024,768]{1,0:T(8,128)(2,1)S(1)} %get-tuple-element.39.tokens.refs_0_, bf16[768,768]{1,0:T(8,128)(2,1)S(1)} %get-tuple-element.54.refs_1_, ...), custom_call_target="tpu_custom_call" | custom-call | flops 3623878656 | tf_op jit(solution)/shard_map/rest_up/pallas_call | solution.py:799
  53.2 0.7 picked_query.1
  53.9 0.0 collective-permute-done.5
  53.9 1.7 %collective-permute-start.6 = (bf16[4,2,16,768]{3,2,1,0:T(8,128)(2,1)S(1)}, bf16[4,2,16,768]{3,2,1,0:T(8,128)(2,1)S(1)}, u32[]{:S(2)}, u32[]{:S(2)}) collective-permute-start(bf16[4,2,16,768]{3,2,1,0:T(8,128)(2,1)S(1)} %constant_dynamic-update-slice_fusion.7.refs_5_), channel_id=1, source_target_pairs={{0,2},{1,5},{2,0},{3,7},{4,6},{5,1},{6,4},{7,3},{8,10},{9,13},{10,... | collective-permute-start | bytes 589832 | tf_op jit(solution)/shard_map/ppermute | solution.py:824
  55.6 4.8 %rest_down.1 = (bf16[768,768]{1,0:T(8,128)(2,1)S(1)}, bf16[4,2,16,768]{3,2,1,0:T(8,128)(2,1)S(1)}) custom-call(bf16[768,768]{1,0:T(8,128)(2,1)S(1)} %get-tuple-element.56.refs_0_, bf16[768,768]{1,0:T(8,128)(2,1)S(1)} %get-tuple-element.57.refs_1_, bf16[768,2304]{1,0:T(8,128)(2,1)S(1)} %get-tuple-element.58.refs_2_, bf16[768,3072]{1,0:T(8,128)(2,1)S(1)} %bitcast.1, ...), custom_call_target="tpu_custom_call" | custom-call | flops 4529848320 | tf_op jit(solution)/shard_map/rest_down/pallas_call | solution.py:799
  60.5 0.0 collective-permute-done.6
  60.5 0.9 %collective-permute-start.7 = (bf16[8,2,16,768]{3,2,1,0:T(8,128)(2,1)S(1)}, bf16[8,2,16,768]{3,2,1,0:T(8,128)(2,1)S(1)}, u32[]{:S(2)}, u32[]{:S(2)}) collective-permute-start(bf16[8,2,16,768]{3,2,1,0:T(8,128)(2,1)S(1)} %constant_dynamic-update-slice_fusion.9.refs_5_), channel_id=1, source_target_pairs={{0,1},{1,0},{2,3},{3,2},{4,5},{5,4},{6,7},{7,6},{8,9},{9,8},{10,11... | collective-permute-start | bytes 1179656 | tf_op jit(solution)/shard_map/ppermute | solution.py:21
  61.4 1.7 %rest_query.1 = (bf16[1024,768]{1,0:T(8,128)(2,1)S(1)}, f32[1,128]{1,0:T(1,128)S(1)}, bf16[8,2,16,768]{3,2,1,0:T(8,128)(2,1)S(1)}) custom-call(bf16[256,768]{1,0:T(8,128)(2,1)S(1)} %get-tuple-element.63.refs_0_, f32[1,128]{1,0:T(1,128)S(1)} %get-tuple-element.64.refs_1_, bf16[768,768]{1,0:T(8,128)(2,1)S(1)} %get-tuple-element.62.refs_2_, f32[768]{0:T(1024)S(1)} %copy-done.4, ...), custom_call_target="tpu_custom_call" | custom-call | flops 905969664 | tf_op jit(solution)/shard_map/rest_query/pallas_call | solution.py:799
  63.2 0.0 collective-permute-done.7.refs_6_
  63.2 20.4 %second_attention.1 = bf16[1024,768]{1,0:T(8,128)(2,1)} custom-call(bf16[256,256]{1,0:T(8,128)(2,1)S(1)} %get-tuple-element.37.refs_0_, bf16[256,768]{1,0:T(8,128)(2,1)S(1)} %get-tuple-element.49.refs_1_, bf16[768,768]{1,0:T(8,128)(2,1)S(1)} %get-tuple-element.62.refs_2_, bf16[1024,768]{1,0:T(8,128)(2,1)S(1)} %get-tuple-element.66.refs_3_, ...), custom_call_target="tpu_custom_call" | custom-call | flops 5502926848 | bytes 1179648 | tf_op jit(solution)/shard_map/second_attention/pallas_call | solution.py:799
  (24 shorter events, 0.1 us)
Async XLA Ops:
  0.0 10.7 %copy-start.5 = (bf16[768,768]{1,0:T(8,128)(2,1)S(1)}, bf16[768,768]{1,0:T(8,128)(2,1)}, u32[]{:S(2)}) copy-start(bf16[768,768]{1,0:T(8,128)(2,1)} %refs_1_.4) | copy-start | bytes 3538948
  3.3 5.0 %collective-permute-start = (bf16[1,2,16,768]{3,2,1,0:T(8,128)(2,1)S(1)}, bf16[1,2,16,768]{3,2,1,0:T(8,128)(2,1)S(1)}, u32[]{:S(2)}, u32[]{:S(2)}) collective-permute-start(bf16[1,2,16,768]{3,2,1,0:T(8,128)(2,1)S(1)} %first_keys.1.refs_3_), channel_id=1, source_target_pairs={{0,8},{1,3},{2,10},{3,1},{4,12},{5,7},{6,14},{7,5},{8,0},{9,11},{1... | collective-permute-start | bytes 147464 | tf_op jit(solution)/shard_map/ppermute | solution.py:824
  5.4 17.2 %slice-start = ((s8[4718592]{0:T(1024)(128)(4,1)}), s8[4194304]{0:T(1024)(128)(4,1)S(1)}, s32[]{:S(2)}) async-start(s8[4718592]{0:T(1024)(128)(4,1)} %bitcast), calls=%async_computation | async-start | bytes 8388608
  8.3 4.4 %collective-permute-start.1 = (bf16[2,2,16,768]{3,2,1,0:T(8,128)(2,1)S(1)}, bf16[2,2,16,768]{3,2,1,0:T(8,128)(2,1)S(1)}, u32[]{:S(2)}, u32[]{:S(2)}) collective-permute-start(bf16[2,2,16,768]{3,2,1,0:T(8,128)(2,1)S(1)} %constant_dynamic-update-slice_fusion.refs_2_), channel_id=1, source_target_pairs={{0,4},{1,9},{2,6},{3,11},{4,0},{5,13},{6,2},{7,15},{8,12},{9,1},{1... | collective-permute-start | bytes 294920 | tf_op jit(solution)/shard_map/ppermute | solution.py:824
  10.7 11.9 %slice-start.1 = ((s8[4718592]{0:T(1024)(128)(4,1)}), s8[524288]{0:T(1024)(128)(4,1)S(1)}, s32[]{:S(2)}) async-start(s8[4718592]{0:T(1024)(128)(4,1)} %bitcast), calls=%async_computation.1 | async-start | bytes 1048576
  10.7 11.9 %copy-start.2 = (bf16[768,768]{1,0:T(8,128)(2,1)S(1)}, bf16[768,768]{1,0:T(8,128)(2,1)}, u32[]{:S(2)}) copy-start(bf16[768,768]{1,0:T(8,128)(2,1)} %refs_2_.3) | copy-start | bytes 3538948
  12.8 4.9 %collective-permute-start.2 = (bf16[4,2,16,768]{3,2,1,0:T(8,128)(2,1)S(1)}, bf16[4,2,16,768]{3,2,1,0:T(8,128)(2,1)S(1)}, u32[]{:S(2)}, u32[]{:S(2)}) collective-permute-start(bf16[4,2,16,768]{3,2,1,0:T(8,128)(2,1)S(1)} %pad_maximum_fusion), channel_id=1, source_target_pairs={{0,2},{1,5},{2,0},{3,7},{4,6},{5,1},{6,4},{7,3},{8,10},{9,13},{10,... | collective-permute-start | bytes 589832 | tf_op jit(solution)/shard_map/ppermute | solution.py:824
  14.6 8.0 %copy-start = (bf16[3072,768]{1,0:T(8,128)(2,1)S(1)}, bf16[3072,768]{1,0:T(8,128)(2,1)}, u32[]{:S(2)}) copy-start(bf16[3072,768]{1,0:T(8,128)(2,1)} %refs_4_.4) | copy-start | bytes 14155780
  17.7 4.9 %collective-permute-start.3 = (bf16[8,2,16,768]{3,2,1,0:T(8,128)(2,1)S(1)}, bf16[8,2,16,768]{3,2,1,0:T(8,128)(2,1)S(1)}, u32[]{:S(2)}, u32[]{:S(2)}) collective-permute-start(bf16[8,2,16,768]{3,2,1,0:T(8,128)(2,1)S(1)} %constant_dynamic-update-slice_fusion.2.keyval.refs_3_), channel_id=1, source_target_pairs={{0,1},{1,0},{2,3},{3,2},{4,5},{5,4},{6,7},{7,6},{8,9},{9,8},{10,11... | collective-permute-start | bytes 1179656 | tf_op jit(solution)/shard_map/ppermute | solution.py:21
  20.9 1.7 %copy-start.3 = (f32[768]{0:T(1024)S(1)}, f32[768]{0:T(1024)}, u32[]{:S(2)}) copy-start(f32[768]{0:T(1024)} %refs_3_.3) | copy-start | bytes 9220
  20.9 1.7 %copy-start.4 = (f32[768]{0:T(1024)S(1)}, f32[768]{0:T(1024)}, u32[]{:S(2)}) copy-start(f32[768]{0:T(1024)} %refs_3_.5) | copy-start | bytes 9220
  32.4 14.3 %collective-permute-start.4 = (bf16[1,2,16,768]{3,2,1,0:T(8,128)(2,1)S(1)}, bf16[1,2,16,768]{3,2,1,0:T(8,128)(2,1)S(1)}, u32[]{:S(2)}, u32[]{:S(2)}) collective-permute-start(bf16[1,2,16,768]{3,2,1,0:T(8,128)(2,1)S(1)} %get-tuple-element.53.refs_8_), channel_id=1, source_target_pairs={{0,8},{1,3},{2,10},{3,1},{4,12},{5,7},{6,14},{7,5},{8,0},{9,11},{1... | collective-permute-start | bytes 147464 | tf_op jit(solution)/shard_map/ppermute | solution.py:824
  46.7 7.2 %collective-permute-start.5 = (bf16[2,2,16,768]{3,2,1,0:T(8,128)(2,1)S(1)}, bf16[2,2,16,768]{3,2,1,0:T(8,128)(2,1)S(1)}, u32[]{:S(2)}, u32[]{:S(2)}) collective-permute-start(bf16[2,2,16,768]{3,2,1,0:T(8,128)(2,1)S(1)} %constant_dynamic-update-slice_fusion.5.refs_5_), channel_id=1, source_target_pairs={{0,4},{1,9},{2,6},{3,11},{4,0},{5,13},{6,2},{7,15},{8,12},{9,1},{1... | collective-permute-start | bytes 294920 | tf_op jit(solution)/shard_map/ppermute | solution.py:824
  48.5 4.7 %copy-start.1 = (bf16[768,768]{1,0:T(8,128)(2,1)S(1)}, bf16[768,768]{1,0:T(8,128)(2,1)}, u32[]{:S(2)}) copy-start(bf16[768,768]{1,0:T(8,128)(2,1)} %refs_4_.5) | copy-start | bytes 3538948
  53.9 6.6 %collective-permute-start.6 = (bf16[4,2,16,768]{3,2,1,0:T(8,128)(2,1)S(1)}, bf16[4,2,16,768]{3,2,1,0:T(8,128)(2,1)S(1)}, u32[]{:S(2)}, u32[]{:S(2)}) collective-permute-start(bf16[4,2,16,768]{3,2,1,0:T(8,128)(2,1)S(1)} %constant_dynamic-update-slice_fusion.7.refs_5_), channel_id=1, source_target_pairs={{0,2},{1,5},{2,0},{3,7},{4,6},{5,1},{6,4},{7,3},{8,10},{9,13},{10,... | collective-permute-start | bytes 589832 | tf_op jit(solution)/shard_map/ppermute | solution.py:824
  60.5 2.7 %collective-permute-start.7 = (bf16[8,2,16,768]{3,2,1,0:T(8,128)(2,1)S(1)}, bf16[8,2,16,768]{3,2,1,0:T(8,128)(2,1)S(1)}, u32[]{:S(2)}, u32[]{:S(2)}) collective-permute-start(bf16[8,2,16,768]{3,2,1,0:T(8,128)(2,1)S(1)} %constant_dynamic-update-slice_fusion.9.refs_5_), channel_id=1, source_target_pairs={{0,1},{1,0},{2,3},{3,2},{4,5},{5,4},{6,7},{7,6},{8,9},{9,8},{10,11... | collective-permute-start | bytes 1179656 | tf_op jit(solution)/shard_map/ppermute | solution.py:21
where the time goes:
time: 84 us; the launch traced here: 83.8 us
  Pallas kernels  64.4 us (77%)
  starting transfers between devices  15.3 us (18%)
  waiting for transfers between devices  3.48 us (4%)
    pallas_call x11, Pallas kernels, local_call(): pl.pallas_call(kernel, out_shape=outs, in_specs=specs, out_specs=[pl.Bloc...  64.4 us
    ppermute x6, starting transfers between devices, exchange(): partner = lax.ppermute(keyval, 'seq', pairs)  11.1 us
    ppermute x2, starting transfers between devices, swapped(): lax.ppermute(x, axis, [(i, i ^ 1 << apart) for i in range(lax.axis_size(a...  4.17 us
    ppermute x6, waiting for transfers between devices, exchange(): partner = lax.ppermute(keyval, 'seq', pairs)  3.48 us
  transfers between devices with their start and end apart: 8, of which 2 were waited for; matrix products, arithmetic and copies ran while one was open for 0% of the time, Pallas kernels for 37%

commit v1 on v0

--- a/solution.py
+++ b/solution.py
@@ -489,13 +489,18 @@
             mixed = dot(weights, values)
             for offset in range(0, size, 128):
                 own = mixed[:, offset : offset + 128]
-                own = own * reciprocal(pltpu.roll(own, 64, 1))
+                total = pltpu.roll(own, 64, 1)
                 at = start + offset
                 if at in sums:
-                    own = jnp.where(lane >= h * head_size - at, own, sums[at])
-                sums[at] = own
+                    mine = lane >= h * head_size - at
+                    own = jnp.where(mine, own, sums[at][0])
+                    total = jnp.where(mine, total, sums[at][1])
+                sums[at] = own, total
                 if (h + 1) * head_size >= at + 128:
-                    mixed_ref[out_span, pl.ds(base + at, 128)] = sums.pop(at).astype(BF16)
+                    own, total = sums.pop(at)
+                    mixed_ref[out_span, pl.ds(base + at, 128)] = (
+                        own * reciprocal(total)
+                    ).astype(BF16)
 
         count = len(windows) // step
         score(0)
@@ -827,6 +832,21 @@
     return beside(levels - 1, keyval), far
 
 
+def early_exchange(keyval, span, beside):
+    levels = span.bit_length() - 1
+    crossed, fresh = [], keyval
+    for level in range(levels - 1, 1, -1):
+        crossed.append(swapped(fresh, "seq", 1))
+        partner = swapped(keyval, "seq", level)
+        keyval = jnp.concatenate([beside(levels - 1 - level, keyval), partner], axis=0)
+        fresh = partner
+    if levels > 1:
+        crossed.append(swapped(fresh, "seq", 1))
+        keyval = jnp.concatenate([beside(levels - 2, keyval), *crossed], axis=0)
+    far = swapped(keyval, "seq", 0)
+    return beside(levels - 1, keyval), far
+
+
 def whole_body(
     tokens,
     attn_gain,
@@ -920,7 +940,7 @@
             )
         return held
 
-    keyval, keyval_far = exchange(keyval, seg_span, beside_first)
+    keyval, keyval_far = early_exchange(keyval, seg_span, beside_first)
     rows = made["rows"]
     query_peaks, near_held = made["peaks"], (made["turned"], made["key_peaks"])
     row_flops = 2 * width * (2 * hidden + width) + 4 * 256 * KEYS * heads

time: 84 us -> 82.7 us (0.985)
    ppermute x6 -> x3, starting transfers between devices: 11.1 us -> 3.3 us  [exchange(): partner = lax.ppermute(keyval, 'seq', pairs)]
    ppermute x2 -> x7, starting transfers between devices: 4.17 us -> 11.7 us  [swapped(): lax.ppermute(x, axis, [(i, i ^ 1 << apart) for i in range(lax.axis_size(a...]
    ppermute x6 -> x3, waiting for transfers between devices: 3.48 us -> 0.01 us  [exchange(): partner = lax.ppermute(keyval, 'seq', pairs)]
    ppermute x2 -> x7, waiting for transfers between devices: 0.01 us -> 2.64 us  [swapped(): lax.ppermute(x, axis, [(i, i ^ 1 << apart) for i in range(lax.axis_size(a...]
  transfers between devices with their start and end apart: 8 -> 10, of which waited for: 2 -> 3; matrix products, arithmetic and copies ran while one was open for 0% -> 0% of each run, Pallas kernels for 37% -> 38%
where the time goes in v1:
time: 82.7 us; the launch traced here: 82.5 us
  Pallas kernels  64.3 us (78%)
  starting transfers between devices  15 us (18%)
  waiting for transfers between devices  2.65 us (3%)
    pallas_call x11, Pallas kernels, local_call(): pl.pallas_call(kernel, out_shape=outs, in_specs=specs, out_specs=[pl.Bloc...  64.3 us
    ppermute x7, starting transfers between devices, swapped(): lax.ppermute(x, axis, [(i, i ^ 1 << apart) for i in range(lax.axis_size(a...  11.7 us
    ppermute x3, starting transfers between devices, exchange(): partner = lax.ppermute(keyval, 'seq', pairs)  3.3 us
    ppermute x7, waiting for transfers between devices, swapped(): lax.ppermute(x, axis, [(i, i ^ 1 << apart) for i in range(lax.axis_size(a...  2.64 us
  transfers between devices with their start and end apart: 10, of which 3 were waited for; matrix products, arithmetic and copies ran while one was open for 0% of the time, Pallas kernels for 38%

profile of v1, /device:TPU:1, one launch (start us, length us, event | category | flops | bytes accessed | tf_op | source)
XLA Modules:
  0.0 82.5 jit_solution(9528471821935476482)
XLA Ops:
  0.0 3.2 %first_keys.1.refs_3_ = bf16[1,2,16,768]{3,2,1,0:T(8,128)(2,1)S(1)} custom-call(s32[16]{0:T(128)} %offsets.1, bf16[1024,768]{1,0:T(8,128)(2,1)} %refs_1_.3, f32[768]{0:T(1024)} %refs_2_.2, bf16[768,768]{1,0:T(8,128)(2,1)} %key_weight.2, bf16[768,768]{1,0:T(8,128)(2,1)} %value_weight.2), custom_call_target="tpu_custom_call" | custom-call | flops 1006632960 | bytes 3935296 | tf_op jit(solution)/shard_map/first_keys/pallas_call | solution.py:804
  3.3 3.2 %collective-permute-start = (bf16[1,2,16,768]{3,2,1,0:T(8,128)(2,1)S(1)}, bf16[1,2,16,768]{3,2,1,0:T(8,128)(2,1)S(1)}, u32[]{:S(2)}, u32[]{:S(2)}) collective-permute-start(bf16[1,2,16,768]{3,2,1,0:T(8,128)(2,1)S(1)} %first_keys.1.refs_3_), channel_id=1, source_target_pairs={{0,8},{1,9},{2,10},{3,11},{4,12},{5,13},{6,14},{7,15},{8,0},{9,1},... | collective-permute-start | bytes 147464 | tf_op jit(solution)/shard_map/ppermute | solution.py:21
  6.5 1.2 %collective-permute-start.2 = (bf16[1,2,16,768]{3,2,1,0:T(8,128)(2,1)S(1)}, bf16[1,2,16,768]{3,2,1,0:T(8,128)(2,1)S(1)}, u32[]{:S(2)}, u32[]{:S(2)}) collective-permute-start(bf16[1,2,16,768]{3,2,1,0:T(8,128)(2,1)S(1)} %first_keys.1.refs_3_), channel_id=1, source_target_pairs={{0,2},{1,3},{2,0},{3,1},{4,6},{5,7},{6,4},{7,5},{8,10},{9,11},{10,... | collective-permute-start | bytes 147464 | tf_op jit(solution)/shard_map/ppermute | solution.py:21
  7.7 2.9 %order.1 = (bf16[1024,768]{1,0:T(8,128)(2,1)S(1)}, bf16[1024,768]{1,0:T(8,128)(2,1)S(1)}, bf16[256,256]{1,0:T(8,128)(2,1)S(1)}, bf16[256,256]{1,0:T(8,128)(2,1)S(1)}, bf16[1,2,16,768]{3,2,1,0:T(8,128)(2,1)S(1)}) custom-call(s32[16]{0:T(128)} %refs_0_.1, bf16[1024,768]{1,0:T(8,128)(2,1)} %refs_1_.3, f32[768]{0:T(1024)} %refs_2_.2, ...), custom_call_target="tpu_custom_call" | custom-call | flops 402653184 | bytes 1576000 | tf_op jit(solution)/shard_map/order/pallas_call | solution.py:804
  10.6 0.0 collective-permute-done
  10.6 1.4 %collective-permute-start.1 = (bf16[2,2,16,768]{3,2,1,0:T(8,128)(2,1)S(1)}, bf16[2,2,16,768]{3,2,1,0:T(8,128)(2,1)S(1)}, u32[]{:S(2)}, u32[]{:S(2)}) collective-permute-start(bf16[2,2,16,768]{3,2,1,0:T(8,128)(2,1)S(1)} %constant_dynamic-update-slice_fusion.refs_2_), channel_id=1, source_target_pairs={{0,4},{1,5},{2,6},{3,7},{4,0},{5,1},{6,2},{7,3},{8,12},{9,13},{10,... | collective-permute-start | bytes 294920 | tf_op jit(solution)/shard_map/ppermute | solution.py:21
  12.0 0.0 copy-done.5
  12.0 1.6 %first_query.1 = (bf16[256,768]{1,0:T(8,128)(2,1)S(1)}, bf16[768,768]{1,0:T(8,128)(2,1)S(1)}, f32[1,128]{1,0:T(1,128)S(1)}, bf16[2,2,16,768]{3,2,1,0:T(8,128)(2,1)S(1)}) custom-call(bf16[1024,768]{1,0:T(8,128)(2,1)S(1)} %get-tuple-element.40.refs_0_, bf16[768,768]{1,0:T(8,128)(2,1)S(1)} %copy-done.5, ...), custom_call_target="tpu_custom_call" | custom-call | flops 1207959552 | tf_op jit(solution)/shard_map/first_query/pallas_call | solution.py:804
  13.6 0.3 collective-permute-start.3
  13.9 0.2 collective-permute-done.1
  14.2 1.1 %collective-permute-start.4 = (bf16[2,2,16,768]{3,2,1,0:T(8,128)(2,1)S(1)}, bf16[2,2,16,768]{3,2,1,0:T(8,128)(2,1)S(1)}, u32[]{:S(2)}, u32[]{:S(2)}) collective-permute-start(bf16[2,2,16,768]{3,2,1,0:T(8,128)(2,1)S(1)} %collective-permute-done.1), channel_id=1, source_target_pairs={{0,2},{1,3},{2,0},{3,1},{4,6},{5,7},{6,4},{7,5},{8,10},{9,11},{10,... | collective-permute-start | bytes 294920 | tf_op jit(solution)/shard_map/ppermute | solution.py:21
  15.2 0.0 collective-permute-done.2
  15.3 1.4 %collective-permute-done.3 = bf16[1,2,16,768]{3,2,1,0:T(8,128)(2,1)S(1)} collective-permute-done((bf16[1,2,16,768]{3,2,1,0:T(8,128)(2,1)S(1)}, bf16[1,2,16,768]{3,2,1,0:T(8,128)(2,1)S(1)}, u32[]{:S(2)}, u32[]{:S(2)}) %collective-permute-start.3) | collective-permute-done | bytes 49184 | tf_op jit(solution)/shard_map/ppermute | solution.py:21
  16.6 1.0 %collective-permute-done.4 = bf16[2,2,16,768]{3,2,1,0:T(8,128)(2,1)S(1)} collective-permute-done((bf16[2,2,16,768]{3,2,1,0:T(8,128)(2,1)S(1)}, bf16[2,2,16,768]{3,2,1,0:T(8,128)(2,1)S(1)}, u32[]{:S(2)}, u32[]{:S(2)}) %collective-permute-start.4) | collective-permute-done | bytes 98336 | tf_op jit(solution)/shard_map/ppermute | solution.py:21
  17.7 3.6 %collective-permute-start.5 = (bf16[8,2,16,768]{3,2,1,0:T(8,128)(2,1)S(1)}, bf16[8,2,16,768]{3,2,1,0:T(8,128)(2,1)S(1)}, u32[]{:S(2)}, u32[]{:S(2)}) collective-permute-start(bf16[8,2,16,768]{3,2,1,0:T(8,128)(2,1)S(1)} %constant_dynamic-update-slice_fusion.2.keyval.refs_3_), channel_id=1, source_target_pairs={{0,1},{1,0},{2,3},{3,2},{4,5},{5,4},{6,7},{7,6},{8,9},{9,8},{10,11... | collective-permute-start | bytes 1179656 | tf_op jit(solution)/shard_map/ppermute | solution.py:21
  21.3 1.6 %near_weights.1 = (bf16[16,256,128]{2,1,0:T(8,128)(2,1)S(1)}, bf16[16,768,128]{2,1,0:T(8,128)(2,1)S(1)}, bf16[768,128]{1,0:T(8,128)(2,1)S(1)}, f32[1,128]{1,0:T(1,128)S(1)}) custom-call(bf16[256,768]{1,0:T(8,128)(2,1)S(1)} %get-tuple-element.42.picked.query, bf16[768,768]{1,0:T(8,128)(2,1)S(1)} %get-tuple-element.44.rest.refs_0_, ...), custom_call_target="tpu_custom_call" | custom-call | flops 1073741824 | tf_op jit(solution)/shard_map/near_weights/pallas_call | solution.py:804
  22.9 0.0 collective-permute-done.5.keyval_far.refs_4_
  23.0 9.7 %layer_of_picked.1 = (bf16[256,768]{1,0:T(8,128)(2,1)S(1)}, bf16[256,768]{1,0:T(8,128)(2,1)S(1)}, bf16[1,2,16,768]{3,2,1,0:T(8,128)(2,1)S(1)}, bf16[768,128]{1,0:T(8,128)(2,1)S(1)}, f32[1,128]{1,0:T(1,128)S(1)}) custom-call(bf16[256,256]{1,0:T(8,128)(2,1)S(1)} %get-tuple-element.38.chooser, bf16[1024,768]{1,0:T(8,128)(2,1)S(1)} %get-tuple-element.39.tokens.refs_0_, ...), custom_call_target="tpu_custom_call" | custom-call | flops 3791650816 | bytes 2359296 | tf_op jit(solution)/shard_map/layer_of_picked/pallas_call | solution.py:804
  32.7 0.5 collective-permute-start.6
  33.2 13.0 %rest_attention.1 = (bf16[768,768]{1,0:T(8,128)(2,1)S(1)}, bf16[1,2,16,768]{3,2,1,0:T(8,128)(2,1)S(1)}) custom-call(bf16[768,768]{1,0:T(8,128)(2,1)S(1)} %get-tuple-element.44.rest.refs_0_, f32[1,128]{1,0:T(1,128)S(1)} %get-tuple-element.43.query_peaks.refs_1_, bf16[16,768,128]{2,1,0:T(8,128)(2,1)S(1)} %get-tuple-element.50.refs_2_, ...), custom_call_target="tpu_custom_call" | custom-call | flops 3221225472 | tf_op jit(solution)/shard_map/rest_attention/pallas_call | solution.py:804
  46.2 0.0 collective-permute-done.6
  46.3 1.0 %collective-permute-start.7 = (bf16[2,2,16,768]{3,2,1,0:T(8,128)(2,1)S(1)}, bf16[2,2,16,768]{3,2,1,0:T(8,128)(2,1)S(1)}, u32[]{:S(2)}, u32[]{:S(2)}) collective-permute-start(bf16[2,2,16,768]{3,2,1,0:T(8,128)(2,1)S(1)} %constant_dynamic-update-slice_fusion.7.refs_5_), channel_id=1, source_target_pairs={{0,4},{1,9},{2,6},{3,11},{4,0},{5,13},{6,2},{7,15},{8,12},{9,1},{1... | collective-permute-start | bytes 294920 | tf_op jit(solution)/shard_map/ppermute | solution.py:829
  47.3 4.7 %rest_up.1 = (bf16[768,768]{1,0:T(8,128)(2,1)S(1)}, bf16[768,768]{1,0:T(8,128)(2,1)S(1)}, bf16[768,2304]{1,0:T(8,128)(2,1)S(1)}, bf16[2,2,16,768]{3,2,1,0:T(8,128)(2,1)S(1)}) custom-call(bf16[1024,768]{1,0:T(8,128)(2,1)S(1)} %get-tuple-element.39.tokens.refs_0_, bf16[768,768]{1,0:T(8,128)(2,1)S(1)} %get-tuple-element.54.refs_1_, ...), custom_call_target="tpu_custom_call" | custom-call | flops 3623878656 | tf_op jit(solution)/shard_map/rest_up/pallas_call | solution.py:804
  52.0 0.7 picked_query.1
  52.7 0.0 collective-permute-done.7
  52.7 1.7 %collective-permute-start.8 = (bf16[4,2,16,768]{3,2,1,0:T(8,128)(2,1)S(1)}, bf16[4,2,16,768]{3,2,1,0:T(8,128)(2,1)S(1)}, u32[]{:S(2)}, u32[]{:S(2)}) collective-permute-start(bf16[4,2,16,768]{3,2,1,0:T(8,128)(2,1)S(1)} %constant_dynamic-update-slice_fusion.9.refs_5_), channel_id=1, source_target_pairs={{0,2},{1,5},{2,0},{3,7},{4,6},{5,1},{6,4},{7,3},{8,10},{9,13},{10,... | collective-permute-start | bytes 589832 | tf_op jit(solution)/shard_map/ppermute | solution.py:829
  54.4 4.8 %rest_down.1 = (bf16[768,768]{1,0:T(8,128)(2,1)S(1)}, bf16[4,2,16,768]{3,2,1,0:T(8,128)(2,1)S(1)}) custom-call(bf16[768,768]{1,0:T(8,128)(2,1)S(1)} %get-tuple-element.56.refs_0_, bf16[768,768]{1,0:T(8,128)(2,1)S(1)} %get-tuple-element.57.refs_1_, bf16[768,2304]{1,0:T(8,128)(2,1)S(1)} %get-tuple-element.58.refs_2_, bf16[768,3072]{1,0:T(8,128)(2,1)S(1)} %bitcast.1, ...), custom_call_target="tpu_custom_call" | custom-call | flops 4529848320 | tf_op jit(solution)/shard_map/rest_down/pallas_call | solution.py:804
  59.3 0.0 collective-permute-done.8
  59.3 0.9 %collective-permute-start.9 = (bf16[8,2,16,768]{3,2,1,0:T(8,128)(2,1)S(1)}, bf16[8,2,16,768]{3,2,1,0:T(8,128)(2,1)S(1)}, u32[]{:S(2)}, u32[]{:S(2)}) collective-permute-start(bf16[8,2,16,768]{3,2,1,0:T(8,128)(2,1)S(1)} %constant_dynamic-update-slice_fusion.11.refs_5_), channel_id=1, source_target_pairs={{0,1},{1,0},{2,3},{3,2},{4,5},{5,4},{6,7},{7,6},{8,9},{9,8},{10,11... | collective-permute-start | bytes 1179656 | tf_op jit(solution)/shard_map/ppermute | solution.py:21
  60.2 1.7 %rest_query.1 = (bf16[1024,768]{1,0:T(8,128)(2,1)S(1)}, f32[1,128]{1,0:T(1,128)S(1)}, bf16[8,2,16,768]{3,2,1,0:T(8,128)(2,1)S(1)}) custom-call(bf16[256,768]{1,0:T(8,128)(2,1)S(1)} %get-tuple-element.63.refs_0_, f32[1,128]{1,0:T(1,128)S(1)} %get-tuple-element.64.refs_1_, bf16[768,768]{1,0:T(8,128)(2,1)S(1)} %get-tuple-element.62.refs_2_, f32[768]{0:T(1024)S(1)} %copy-done.4, ...), custom_call_target="tpu_custom_call" | custom-call | flops 905969664 | tf_op jit(solution)/shard_map/rest_query/pallas_call | solution.py:804
  62.0 0.0 collective-permute-done.9.refs_6_
  62.0 20.3 %second_attention.1 = bf16[1024,768]{1,0:T(8,128)(2,1)} custom-call(bf16[256,256]{1,0:T(8,128)(2,1)S(1)} %get-tuple-element.37.refs_0_, bf16[256,768]{1,0:T(8,128)(2,1)S(1)} %get-tuple-element.49.refs_1_, bf16[768,768]{1,0:T(8,128)(2,1)S(1)} %get-tuple-element.62.refs_2_, bf16[1024,768]{1,0:T(8,128)(2,1)S(1)} %get-tuple-element.66.refs_3_, ...), custom_call_target="tpu_custom_call" | custom-call | flops 5502926848 | bytes 1179648 | tf_op jit(solution)/shard_map/second_attention/pallas_call | solution.py:804
  (29 shorter events, 0.1 us)
Async XLA Ops:
  0.0 12.0 %copy-start.5 = (bf16[768,768]{1,0:T(8,128)(2,1)S(1)}, bf16[768,768]{1,0:T(8,128)(2,1)}, u32[]{:S(2)}) copy-start(bf16[768,768]{1,0:T(8,128)(2,1)} %refs_1_.4) | copy-start | bytes 3538948
  3.3 7.4 %collective-permute-start = (bf16[1,2,16,768]{3,2,1,0:T(8,128)(2,1)S(1)}, bf16[1,2,16,768]{3,2,1,0:T(8,128)(2,1)S(1)}, u32[]{:S(2)}, u32[]{:S(2)}) collective-permute-start(bf16[1,2,16,768]{3,2,1,0:T(8,128)(2,1)S(1)} %first_keys.1.refs_3_), channel_id=1, source_target_pairs={{0,8},{1,9},{2,10},{3,11},{4,12},{5,13},{6,14},{7,15},{8,0},{9,1},... | collective-permute-start | bytes 147464 | tf_op jit(solution)/shard_map/ppermute | solution.py:21
  6.5 8.8 %collective-permute-start.2 = (bf16[1,2,16,768]{3,2,1,0:T(8,128)(2,1)S(1)}, bf16[1,2,16,768]{3,2,1,0:T(8,128)(2,1)S(1)}, u32[]{:S(2)}, u32[]{:S(2)}) collective-permute-start(bf16[1,2,16,768]{3,2,1,0:T(8,128)(2,1)S(1)} %first_keys.1.refs_3_), channel_id=1, source_target_pairs={{0,2},{1,3},{2,0},{3,1},{4,6},{5,7},{6,4},{7,5},{8,10},{9,11},{10,... | collective-permute-start | bytes 147464 | tf_op jit(solution)/shard_map/ppermute | solution.py:21
  7.7 15.3 %slice-start = ((s8[4718592]{0:T(1024)(128)(4,1)}), s8[4194304]{0:T(1024)(128)(4,1)S(1)}, s32[]{:S(2)}) async-start(s8[4718592]{0:T(1024)(128)(4,1)} %bitcast), calls=%async_computation | async-start | bytes 8388608
  10.6 3.5 %collective-permute-start.1 = (bf16[2,2,16,768]{3,2,1,0:T(8,128)(2,1)S(1)}, bf16[2,2,16,768]{3,2,1,0:T(8,128)(2,1)S(1)}, u32[]{:S(2)}, u32[]{:S(2)}) collective-permute-start(bf16[2,2,16,768]{3,2,1,0:T(8,128)(2,1)S(1)} %constant_dynamic-update-slice_fusion.refs_2_), channel_id=1, source_target_pairs={{0,4},{1,5},{2,6},{3,7},{4,0},{5,1},{6,2},{7,3},{8,12},{9,13},{10,... | collective-permute-start | bytes 294920 | tf_op jit(solution)/shard_map/ppermute | solution.py:21
  12.0 10.9 %slice-start.1 = ((s8[4718592]{0:T(1024)(128)(4,1)}), s8[524288]{0:T(1024)(128)(4,1)S(1)}, s32[]{:S(2)}) async-start(s8[4718592]{0:T(1024)(128)(4,1)} %bitcast), calls=%async_computation.1 | async-start | bytes 1048576
  12.0 10.9 %copy-start.2 = (bf16[768,768]{1,0:T(8,128)(2,1)S(1)}, bf16[768,768]{1,0:T(8,128)(2,1)}, u32[]{:S(2)}) copy-start(bf16[768,768]{1,0:T(8,128)(2,1)} %refs_2_.3) | copy-start | bytes 3538948
  13.6 3.0 %collective-permute-start.3 = (bf16[1,2,16,768]{3,2,1,0:T(8,128)(2,1)S(1)}, bf16[1,2,16,768]{3,2,1,0:T(8,128)(2,1)S(1)}, u32[]{:S(2)}, u32[]{:S(2)}) collective-permute-start(bf16[1,2,16,768]{3,2,1,0:T(8,128)(2,1)S(1)} %collective-permute-done), channel_id=1, source_target_pairs={{0,2},{1,3},{2,0},{3,1},{4,6},{5,7},{6,4},{7,5},{8,10},{9,11},{10,... | collective-permute-start | bytes 147464 | tf_op jit(solution)/shard_map/ppermute | solution.py:21
  13.9 9.0 %copy-start = (bf16[3072,768]{1,0:T(8,128)(2,1)S(1)}, bf16[3072,768]{1,0:T(8,128)(2,1)}, u32[]{:S(2)}) copy-start(bf16[3072,768]{1,0:T(8,128)(2,1)} %refs_4_.4) | copy-start | bytes 14155780
  14.2 3.5 %collective-permute-start.4 = (bf16[2,2,16,768]{3,2,1,0:T(8,128)(2,1)S(1)}, bf16[2,2,16,768]{3,2,1,0:T(8,128)(2,1)S(1)}, u32[]{:S(2)}, u32[]{:S(2)}) collective-permute-start(bf16[2,2,16,768]{3,2,1,0:T(8,128)(2,1)S(1)} %collective-permute-done.1), channel_id=1, source_target_pairs={{0,2},{1,3},{2,0},{3,1},{4,6},{5,7},{6,4},{7,5},{8,10},{9,11},{10,... | collective-permute-start | bytes 294920 | tf_op jit(solution)/shard_map/ppermute | solution.py:21
  17.7 5.2 %collective-permute-start.5 = (bf16[8,2,16,768]{3,2,1,0:T(8,128)(2,1)S(1)}, bf16[8,2,16,768]{3,2,1,0:T(8,128)(2,1)S(1)}, u32[]{:S(2)}, u32[]{:S(2)}) collective-permute-start(bf16[8,2,16,768]{3,2,1,0:T(8,128)(2,1)S(1)} %constant_dynamic-update-slice_fusion.2.keyval.refs_3_), channel_id=1, source_target_pairs={{0,1},{1,0},{2,3},{3,2},{4,5},{5,4},{6,7},{7,6},{8,9},{9,8},{10,11... | collective-permute-start | bytes 1179656 | tf_op jit(solution)/shard_map/ppermute | solution.py:21
  21.3 1.7 %copy-start.3 = (f32[768]{0:T(1024)S(1)}, f32[768]{0:T(1024)}, u32[]{:S(2)}) copy-start(f32[768]{0:T(1024)} %refs_3_.3) | copy-start | bytes 9220
  21.3 1.7 %copy-start.4 = (f32[768]{0:T(1024)S(1)}, f32[768]{0:T(1024)}, u32[]{:S(2)}) copy-start(f32[768]{0:T(1024)} %refs_3_.5) | copy-start | bytes 9220
  32.7 13.5 %collective-permute-start.6 = (bf16[1,2,16,768]{3,2,1,0:T(8,128)(2,1)S(1)}, bf16[1,2,16,768]{3,2,1,0:T(8,128)(2,1)S(1)}, u32[]{:S(2)}, u32[]{:S(2)}) collective-permute-start(bf16[1,2,16,768]{3,2,1,0:T(8,128)(2,1)S(1)} %get-tuple-element.53.refs_8_), channel_id=1, source_target_pairs={{0,8},{1,3},{2,10},{3,1},{4,12},{5,7},{6,14},{7,5},{8,0},{9,11},{1... | collective-permute-start | bytes 147464 | tf_op jit(solution)/shard_map/ppermute | solution.py:829
  46.3 6.4 %collective-permute-start.7 = (bf16[2,2,16,768]{3,2,1,0:T(8,128)(2,1)S(1)}, bf16[2,2,16,768]{3,2,1,0:T(8,128)(2,1)S(1)}, u32[]{:S(2)}, u32[]{:S(2)}) collective-permute-start(bf16[2,2,16,768]{3,2,1,0:T(8,128)(2,1)S(1)} %constant_dynamic-update-slice_fusion.7.refs_5_), channel_id=1, source_target_pairs={{0,4},{1,9},{2,6},{3,11},{4,0},{5,13},{6,2},{7,15},{8,12},{9,1},{1... | collective-permute-start | bytes 294920 | tf_op jit(solution)/shard_map/ppermute | solution.py:829
  47.3 4.7 %copy-start.1 = (bf16[768,768]{1,0:T(8,128)(2,1)S(1)}, bf16[768,768]{1,0:T(8,128)(2,1)}, u32[]{:S(2)}) copy-start(bf16[768,768]{1,0:T(8,128)(2,1)} %refs_4_.5) | copy-start | bytes 3538948
  52.7 6.6 %collective-permute-start.8 = (bf16[4,2,16,768]{3,2,1,0:T(8,128)(2,1)S(1)}, bf16[4,2,16,768]{3,2,1,0:T(8,128)(2,1)S(1)}, u32[]{:S(2)}, u32[]{:S(2)}) collective-permute-start(bf16[4,2,16,768]{3,2,1,0:T(8,128)(2,1)S(1)} %constant_dynamic-update-slice_fusion.9.refs_5_), channel_id=1, source_target_pairs={{0,2},{1,5},{2,0},{3,7},{4,6},{5,1},{6,4},{7,3},{8,10},{9,13},{10,... | collective-permute-start | bytes 589832 | tf_op jit(solution)/shard_map/ppermute | solution.py:829
  59.3 2.7 %collective-permute-start.9 = (bf16[8,2,16,768]{3,2,1,0:T(8,128)(2,1)S(1)}, bf16[8,2,16,768]{3,2,1,0:T(8,128)(2,1)S(1)}, u32[]{:S(2)}, u32[]{:S(2)}) collective-permute-start(bf16[8,2,16,768]{3,2,1,0:T(8,128)(2,1)S(1)} %constant_dynamic-update-slice_fusion.11.refs_5_), channel_id=1, source_target_pairs={{0,1},{1,0},{2,3},{3,2},{4,5},{5,4},{6,7},{7,6},{8,9},{9,8},{10,11... | collective-permute-start | bytes 1179656 | tf_op jit(solution)/shard_map/ppermute | solution.py:21

commit v2 on v1

--- a/solution.py
+++ b/solution.py
@@ -319,13 +319,15 @@
     norm_into(normed, 0, moved_rows, scale[...], count)
 
 
-def scaled_query(normed, weight, outs, heads, peaks):
-    width = normed.shape[1]
-    factor = (width // heads) ** (-0.5) * LOG2E
+def score_scale(head_size):
+    return head_size ** (-0.5) * LOG2E
+
+
+def project_query(normed, weight, outs, heads, peaks):
     peak = None
     for out, row in outs:
         for span in pieces(out.shape[0], 512 if out.shape[0] % 512 == 0 else 256):
-            query = dot(normed[row + span.start : row + span.stop, :], weight[...]) * factor
+            query = dot(normed[row + span.start : row + span.stop, :], weight[...])
             out[span, :] = query.astype(BF16)
             for part in pieces(query.shape[0], 64):
                 square = query[part] * query[part]
@@ -335,7 +337,7 @@
 
 def first_query_kernel(normed, weight, picked, rest, peaks, sems, *, heads):
     del sems
-    scaled_query(normed, weight, [(picked, 0), (rest, picked.shape[0])], heads, peaks)
+    project_query(normed, weight, [(picked, 0), (rest, picked.shape[0])], heads, peaks)
 
 
 def head_windows(head_size, width):
@@ -363,8 +365,9 @@
     return keys * keys
 
 
-def small_scores(query_peaks, key_peaks):
-    return jnp.max(query_peaks[...] * key_peaks[...]) < 9000.0
+def small_scores(query_peaks, key_peaks, head_size):
+    scale = score_scale(head_size)
+    return jnp.max(query_peaks[...] * key_peaks[...]) < 9000.0 / (scale * scale)
 
 
 def reciprocal(x):
@@ -399,6 +402,7 @@
     peaks[...] = summed_peaks(load_keys(keyval, turned), heads)
     width = picked.shape[1]
     head_size = width // heads
+    scale = score_scale(head_size)
     key_count = turned.shape[1]
     period, windows = head_windows(head_size, width)
     jobs = [
@@ -423,7 +427,7 @@
             if i + 1 < len(jobs):
                 score(i + 1)
             for part in pieces(query.shape[0], 64):
-                weights = jnp.exp2(scores_ref[i % 2, part, :]).astype(BF16)
+                weights = jnp.exp2(scores_ref[i % 2, part, :] * scale).astype(BF16)
                 for j in range(2):
                     early[turn * len(windows) + head + j, part, :] = weights[
                         :, j * key_count : (j + 1) * key_count
@@ -440,6 +444,7 @@
     period, windows = head_windows(head_size, width)
     span = pl.ds(first_row, rows)
     out_span = pl.ds(mixed_row, rows)
+    scale = score_scale(head_size)
     lane = lax.broadcasted_iota(jnp.int32, (1, 128), 1)
     step = 2 if early is not None else 1
 
@@ -463,7 +468,7 @@
                 scores = scores_ref[h % 2, part, :]
                 if not plain:
                     scores = scores - jnp.max(scores, axis=1, keepdims=True)
-                weights_ref[h % 2, part, :] = jnp.exp2(scores).astype(BF16)
+                weights_ref[h % 2, part, :] = jnp.exp2(scores * scale).astype(BF16)
 
         def mix(h):
             start, size = windows[h]
@@ -648,7 +653,7 @@
     keyvals = (keyval, keyval_far)
     squares = load_keys(keyval_far, turned)
     peaks[...] = jnp.maximum(peaks_near[...], summed_peaks(squares, heads))
-    small = small_scores(query_peaks, peaks)
+    small = small_scores(query_peaks, peaks, query.shape[1] // heads)
     attend(
         query,
         rows,
@@ -701,7 +706,7 @@
         (keyval, keyval_far),
         mixed,
         (scores, weights),
-        small_scores(query_peaks, peaks),
+        small_scores(query_peaks, peaks, query.shape[1] // heads),
         early,
     )
 
@@ -726,7 +731,7 @@
 
 def picked_query_kernel(normed, weight, query, peaks, sems, *, heads):
     del sems
-    scaled_query(normed, weight, [(query, 0)], heads, peaks)
+    project_query(normed, weight, [(query, 0)], heads, peaks)
 
 
 def rest_query_kernel(
@@ -737,7 +742,7 @@
     query[:start, :] = picked[...]
     norm_into(normed, 0, rows, gain[...], rows.shape[0])
     out = query.at[pl.ds(start, rows.shape[0])]
-    scaled_query(normed, weight, [(out, 0)], heads, peaks)
+    project_query(normed, weight, [(out, 0)], heads, peaks)
     peaks[...] = jnp.maximum(peaks[...], picked_peaks[...])
 
 
@@ -750,7 +755,7 @@
     keyvals = (keyval, keyval_far)
     squares = jnp.maximum(load_keys(keyval, turned_near), load_keys(keyval_far, turned))
     count = query.shape[0]
-    small = small_scores(query_peaks, summed_peaks(squares, heads))
+    small = small_scores(query_peaks, summed_peaks(squares, heads), query.shape[1] // heads)
     attend(
         query, count, heads, (turned_near, turned), keyvals, mixed, (scores, weights), small
     )
@@ -1052,7 +1057,7 @@
         )
         return held
 
-    tasks = [[rest_attention], [rest_up, picked_query], [rest_down], [rest_query]]
+    tasks = [[rest_attention, picked_query], [rest_up], [rest_down], [rest_query]]
     levels = seq_count.bit_length() - 1
 
     def beside_second(level, held):

time: 82.7 us -> 83.4 us (level)
  no operation moved by 1% of the time
where the time goes in v2:
time: 83.4 us; the launch traced here: 83.2 us
  Pallas kernels  65 us (78%)
  starting transfers between devices  15 us (18%)
  waiting for transfers between devices  2.67 us (3%)
    pallas_call x11, Pallas kernels, local_call(): pl.pallas_call(kernel, out_shape=outs, in_specs=specs, out_specs=[pl.Bloc...  65 us
    ppermute x7, starting transfers between devices, swapped(): lax.ppermute(x, axis, [(i, i ^ 1 << apart) for i in range(lax.axis_size(a...  11.7 us
    ppermute x3, starting transfers between devices, exchange(): partner = lax.ppermute(keyval, 'seq', pairs)  3.3 us
    ppermute x7, waiting for transfers between devices, swapped(): lax.ppermute(x, axis, [(i, i ^ 1 << apart) for i in range(lax.axis_size(a...  2.66 us
  transfers between devices with their start and end apart: 10, of which 3 were waited for; matrix products, arithmetic and copies ran while one was open for 0% of the time, Pallas kernels for 38%

profile of v2, /device:TPU:1, one launch (start us, length us, event | category | flops | bytes accessed | tf_op | source)
XLA Modules:
  0.0 83.2 jit_solution(13926599961781607467)
XLA Ops:
  0.0 3.2 %first_keys.1.refs_3_ = bf16[1,2,16,768]{3,2,1,0:T(8,128)(2,1)S(1)} custom-call(s32[16]{0:T(128)} %offsets.1, bf16[1024,768]{1,0:T(8,128)(2,1)} %refs_1_.3, f32[768]{0:T(1024)} %refs_2_.2, bf16[768,768]{1,0:T(8,128)(2,1)} %key_weight.2, bf16[768,768]{1,0:T(8,128)(2,1)} %value_weight.2), custom_call_target="tpu_custom_call" | custom-call | flops 1006632960 | bytes 3935296 | tf_op jit(solution)/shard_map/first_keys/pallas_call | solution.py:809
  3.3 3.2 %collective-permute-start = (bf16[1,2,16,768]{3,2,1,0:T(8,128)(2,1)S(1)}, bf16[1,2,16,768]{3,2,1,0:T(8,128)(2,1)S(1)}, u32[]{:S(2)}, u32[]{:S(2)}) collective-permute-start(bf16[1,2,16,768]{3,2,1,0:T(8,128)(2,1)S(1)} %first_keys.1.refs_3_), channel_id=1, source_target_pairs={{0,8},{1,9},{2,10},{3,11},{4,12},{5,13},{6,14},{7,15},{8,0},{9,1},... | collective-permute-start | bytes 147464 | tf_op jit(solution)/shard_map/ppermute | solution.py:21
  6.5 1.2 %collective-permute-start.2 = (bf16[1,2,16,768]{3,2,1,0:T(8,128)(2,1)S(1)}, bf16[1,2,16,768]{3,2,1,0:T(8,128)(2,1)S(1)}, u32[]{:S(2)}, u32[]{:S(2)}) collective-permute-start(bf16[1,2,16,768]{3,2,1,0:T(8,128)(2,1)S(1)} %first_keys.1.refs_3_), channel_id=1, source_target_pairs={{0,2},{1,3},{2,0},{3,1},{4,6},{5,7},{6,4},{7,5},{8,10},{9,11},{10,... | collective-permute-start | bytes 147464 | tf_op jit(solution)/shard_map/ppermute | solution.py:21
  7.7 2.9 %order.1 = (bf16[1024,768]{1,0:T(8,128)(2,1)S(1)}, bf16[1024,768]{1,0:T(8,128)(2,1)S(1)}, bf16[256,256]{1,0:T(8,128)(2,1)S(1)}, bf16[256,256]{1,0:T(8,128)(2,1)S(1)}, bf16[1,2,16,768]{3,2,1,0:T(8,128)(2,1)S(1)}) custom-call(s32[16]{0:T(128)} %refs_0_.1, bf16[1024,768]{1,0:T(8,128)(2,1)} %refs_1_.3, f32[768]{0:T(1024)} %refs_2_.2, ...), custom_call_target="tpu_custom_call" | custom-call | flops 402653184 | bytes 1576000 | tf_op jit(solution)/shard_map/order/pallas_call | solution.py:809
  10.6 0.0 collective-permute-done
  10.6 1.4 %collective-permute-start.1 = (bf16[2,2,16,768]{3,2,1,0:T(8,128)(2,1)S(1)}, bf16[2,2,16,768]{3,2,1,0:T(8,128)(2,1)S(1)}, u32[]{:S(2)}, u32[]{:S(2)}) collective-permute-start(bf16[2,2,16,768]{3,2,1,0:T(8,128)(2,1)S(1)} %constant_dynamic-update-slice_fusion.refs_2_), channel_id=1, source_target_pairs={{0,4},{1,5},{2,6},{3,7},{4,0},{5,1},{6,2},{7,3},{8,12},{9,13},{10,... | collective-permute-start | bytes 294920 | tf_op jit(solution)/shard_map/ppermute | solution.py:21
  12.0 0.0 copy-done.5
  12.0 1.6 %first_query.1 = (bf16[256,768]{1,0:T(8,128)(2,1)S(1)}, bf16[768,768]{1,0:T(8,128)(2,1)S(1)}, f32[1,128]{1,0:T(1,128)S(1)}, bf16[2,2,16,768]{3,2,1,0:T(8,128)(2,1)S(1)}) custom-call(bf16[1024,768]{1,0:T(8,128)(2,1)S(1)} %get-tuple-element.40.refs_0_, bf16[768,768]{1,0:T(8,128)(2,1)S(1)} %copy-done.5, ...), custom_call_target="tpu_custom_call" | custom-call | flops 1207959552 | tf_op jit(solution)/shard_map/first_query/pallas_call | solution.py:809
  13.6 0.3 collective-permute-start.3
  13.9 0.2 collective-permute-done.1
  14.2 1.0 %collective-permute-start.4 = (bf16[2,2,16,768]{3,2,1,0:T(8,128)(2,1)S(1)}, bf16[2,2,16,768]{3,2,1,0:T(8,128)(2,1)S(1)}, u32[]{:S(2)}, u32[]{:S(2)}) collective-permute-start(bf16[2,2,16,768]{3,2,1,0:T(8,128)(2,1)S(1)} %collective-permute-done.1), channel_id=1, source_target_pairs={{0,2},{1,3},{2,0},{3,1},{4,6},{5,7},{6,4},{7,5},{8,10},{9,11},{10,... | collective-permute-start | bytes 294920 | tf_op jit(solution)/shard_map/ppermute | solution.py:21
  15.2 0.0 collective-permute-done.2
  15.2 1.4 %collective-permute-done.3 = bf16[1,2,16,768]{3,2,1,0:T(8,128)(2,1)S(1)} collective-permute-done((bf16[1,2,16,768]{3,2,1,0:T(8,128)(2,1)S(1)}, bf16[1,2,16,768]{3,2,1,0:T(8,128)(2,1)S(1)}, u32[]{:S(2)}, u32[]{:S(2)}) %collective-permute-start.3) | collective-permute-done | bytes 49184 | tf_op jit(solution)/shard_map/ppermute | solution.py:21
  16.6 1.0 %collective-permute-done.4 = bf16[2,2,16,768]{3,2,1,0:T(8,128)(2,1)S(1)} collective-permute-done((bf16[2,2,16,768]{3,2,1,0:T(8,128)(2,1)S(1)}, bf16[2,2,16,768]{3,2,1,0:T(8,128)(2,1)S(1)}, u32[]{:S(2)}, u32[]{:S(2)}) %collective-permute-start.4) | collective-permute-done | bytes 98336 | tf_op jit(solution)/shard_map/ppermute | solution.py:21
  17.7 3.6 %collective-permute-start.5 = (bf16[8,2,16,768]{3,2,1,0:T(8,128)(2,1)S(1)}, bf16[8,2,16,768]{3,2,1,0:T(8,128)(2,1)S(1)}, u32[]{:S(2)}, u32[]{:S(2)}) collective-permute-start(bf16[8,2,16,768]{3,2,1,0:T(8,128)(2,1)S(1)} %constant_dynamic-update-slice_fusion.2.keyval.refs_3_), channel_id=1, source_target_pairs={{0,1},{1,0},{2,3},{3,2},{4,5},{5,4},{6,7},{7,6},{8,9},{9,8},{10,11... | collective-permute-start | bytes 1179656 | tf_op jit(solution)/shard_map/ppermute | solution.py:21
  21.3 1.7 %near_weights.1 = (bf16[16,256,128]{2,1,0:T(8,128)(2,1)S(1)}, bf16[16,768,128]{2,1,0:T(8,128)(2,1)S(1)}, bf16[768,128]{1,0:T(8,128)(2,1)S(1)}, f32[1,128]{1,0:T(1,128)S(1)}) custom-call(bf16[256,768]{1,0:T(8,128)(2,1)S(1)} %get-tuple-element.42.picked.query, bf16[768,768]{1,0:T(8,128)(2,1)S(1)} %get-tuple-element.44.rest.refs_0_, ...), custom_call_target="tpu_custom_call" | custom-call | flops 1073741824 | tf_op jit(solution)/shard_map/near_weights/pallas_call | solution.py:809
  22.9 0.0 collective-permute-done.5.keyval_far.refs_4_
  23.0 9.8 %layer_of_picked.1 = (bf16[256,768]{1,0:T(8,128)(2,1)S(1)}, bf16[256,768]{1,0:T(8,128)(2,1)S(1)}, bf16[1,2,16,768]{3,2,1,0:T(8,128)(2,1)S(1)}, bf16[768,128]{1,0:T(8,128)(2,1)S(1)}, f32[1,128]{1,0:T(1,128)S(1)}) custom-call(bf16[256,256]{1,0:T(8,128)(2,1)S(1)} %get-tuple-element.38.chooser, bf16[1024,768]{1,0:T(8,128)(2,1)S(1)} %get-tuple-element.39.tokens.refs_0_, ...), custom_call_target="tpu_custom_call" | custom-call | flops 3791650816 | bytes 2359296 | tf_op jit(solution)/shard_map/layer_of_picked/pallas_call | solution.py:809
  32.8 0.5 collective-permute-start.6
  33.3 13.3 %rest_attention.1 = (bf16[768,768]{1,0:T(8,128)(2,1)S(1)}, bf16[1,2,16,768]{3,2,1,0:T(8,128)(2,1)S(1)}) custom-call(bf16[768,768]{1,0:T(8,128)(2,1)S(1)} %get-tuple-element.44.rest.refs_0_, f32[1,128]{1,0:T(1,128)S(1)} %get-tuple-element.43.query_peaks.refs_1_, bf16[16,768,128]{2,1,0:T(8,128)(2,1)S(1)} %get-tuple-element.50.refs_2_, ...), custom_call_target="tpu_custom_call" | custom-call | flops 3221225472 | tf_op jit(solution)/shard_map/rest_attention/pallas_call | solution.py:809
  46.6 0.7 picked_query.1
  47.3 0.0 collective-permute-done.6
  47.3 1.1 %collective-permute-start.7 = (bf16[2,2,16,768]{3,2,1,0:T(8,128)(2,1)S(1)}, bf16[2,2,16,768]{3,2,1,0:T(8,128)(2,1)S(1)}, u32[]{:S(2)}, u32[]{:S(2)}) collective-permute-start(bf16[2,2,16,768]{3,2,1,0:T(8,128)(2,1)S(1)} %constant_dynamic-update-slice_fusion.7.refs_5_), channel_id=1, source_target_pairs={{0,4},{1,9},{2,6},{3,11},{4,0},{5,13},{6,2},{7,15},{8,12},{9,1},{1... | collective-permute-start | bytes 294920 | tf_op jit(solution)/shard_map/ppermute | solution.py:834
  48.3 4.7 %rest_up.1 = (bf16[768,768]{1,0:T(8,128)(2,1)S(1)}, bf16[768,768]{1,0:T(8,128)(2,1)S(1)}, bf16[768,2304]{1,0:T(8,128)(2,1)S(1)}, bf16[2,2,16,768]{3,2,1,0:T(8,128)(2,1)S(1)}) custom-call(bf16[1024,768]{1,0:T(8,128)(2,1)S(1)} %get-tuple-element.39.tokens.refs_0_, bf16[768,768]{1,0:T(8,128)(2,1)S(1)} %get-tuple-element.54.refs_1_, ...), custom_call_target="tpu_custom_call" | custom-call | flops 3623878656 | tf_op jit(solution)/shard_map/rest_up/pallas_call | solution.py:809
  53.0 0.0 collective-permute-done.7
  53.1 1.7 %collective-permute-start.8 = (bf16[4,2,16,768]{3,2,1,0:T(8,128)(2,1)S(1)}, bf16[4,2,16,768]{3,2,1,0:T(8,128)(2,1)S(1)}, u32[]{:S(2)}, u32[]{:S(2)}) collective-permute-start(bf16[4,2,16,768]{3,2,1,0:T(8,128)(2,1)S(1)} %constant_dynamic-update-slice_fusion.9.refs_5_), channel_id=1, source_target_pairs={{0,2},{1,5},{2,0},{3,7},{4,6},{5,1},{6,4},{7,3},{8,10},{9,13},{10,... | collective-permute-start | bytes 589832 | tf_op jit(solution)/shard_map/ppermute | solution.py:834
  54.8 4.8 %rest_down.1 = (bf16[768,768]{1,0:T(8,128)(2,1)S(1)}, bf16[4,2,16,768]{3,2,1,0:T(8,128)(2,1)S(1)}) custom-call(bf16[768,768]{1,0:T(8,128)(2,1)S(1)} %get-tuple-element.58.refs_0_, bf16[768,768]{1,0:T(8,128)(2,1)S(1)} %get-tuple-element.59.refs_1_, bf16[768,2304]{1,0:T(8,128)(2,1)S(1)} %get-tuple-element.60.refs_2_, bf16[768,3072]{1,0:T(8,128)(2,1)S(1)} %bitcast.1, ...), custom_call_target="tpu_custom_call" | custom-call | flops 4529848320 | tf_op jit(solution)/shard_map/rest_down/pallas_call | solution.py:809
  59.7 0.0 collective-permute-done.8
  59.7 0.9 %collective-permute-start.9 = (bf16[8,2,16,768]{3,2,1,0:T(8,128)(2,1)S(1)}, bf16[8,2,16,768]{3,2,1,0:T(8,128)(2,1)S(1)}, u32[]{:S(2)}, u32[]{:S(2)}) collective-permute-start(bf16[8,2,16,768]{3,2,1,0:T(8,128)(2,1)S(1)} %constant_dynamic-update-slice_fusion.11.refs_5_), channel_id=1, source_target_pairs={{0,1},{1,0},{2,3},{3,2},{4,5},{5,4},{6,7},{7,6},{8,9},{9,8},{10,11... | collective-permute-start | bytes 1179656 | tf_op jit(solution)/shard_map/ppermute | solution.py:21
  60.6 1.7 %rest_query.1 = (bf16[1024,768]{1,0:T(8,128)(2,1)S(1)}, f32[1,128]{1,0:T(1,128)S(1)}, bf16[8,2,16,768]{3,2,1,0:T(8,128)(2,1)S(1)}) custom-call(bf16[256,768]{1,0:T(8,128)(2,1)S(1)} %get-tuple-element.63.refs_0_, f32[1,128]{1,0:T(1,128)S(1)} %get-tuple-element.64.refs_1_, bf16[768,768]{1,0:T(8,128)(2,1)S(1)} %get-tuple-element.62.refs_2_, f32[768]{0:T(1024)S(1)} %copy-done.4, ...), custom_call_target="tpu_custom_call" | custom-call | flops 905969664 | tf_op jit(solution)/shard_map/rest_query/pallas_call | solution.py:809
  62.3 0.0 collective-permute-done.9.refs_6_
  62.3 20.7 %second_attention.1 = bf16[1024,768]{1,0:T(8,128)(2,1)} custom-call(bf16[256,256]{1,0:T(8,128)(2,1)S(1)} %get-tuple-element.37.refs_0_, bf16[256,768]{1,0:T(8,128)(2,1)S(1)} %get-tuple-element.49.refs_1_, bf16[768,768]{1,0:T(8,128)(2,1)S(1)} %get-tuple-element.62.refs_2_, bf16[1024,768]{1,0:T(8,128)(2,1)S(1)} %get-tuple-element.66.refs_3_, ...), custom_call_target="tpu_custom_call" | custom-call | flops 5502926848 | bytes 1179648 | tf_op jit(solution)/shard_map/second_attention/pallas_call | solution.py:809
  (29 shorter events, 0.1 us)
Async XLA Ops:
  0.0 12.0 %copy-start.5 = (bf16[768,768]{1,0:T(8,128)(2,1)S(1)}, bf16[768,768]{1,0:T(8,128)(2,1)}, u32[]{:S(2)}) copy-start(bf16[768,768]{1,0:T(8,128)(2,1)} %refs_1_.4) | copy-start | bytes 3538948
  3.3 7.4 %collective-permute-start = (bf16[1,2,16,768]{3,2,1,0:T(8,128)(2,1)S(1)}, bf16[1,2,16,768]{3,2,1,0:T(8,128)(2,1)S(1)}, u32[]{:S(2)}, u32[]{:S(2)}) collective-permute-start(bf16[1,2,16,768]{3,2,1,0:T(8,128)(2,1)S(1)} %first_keys.1.refs_3_), channel_id=1, source_target_pairs={{0,8},{1,9},{2,10},{3,11},{4,12},{5,13},{6,14},{7,15},{8,0},{9,1},... | collective-permute-start | bytes 147464 | tf_op jit(solution)/shard_map/ppermute | solution.py:21
  6.5 8.8 %collective-permute-start.2 = (bf16[1,2,16,768]{3,2,1,0:T(8,128)(2,1)S(1)}, bf16[1,2,16,768]{3,2,1,0:T(8,128)(2,1)S(1)}, u32[]{:S(2)}, u32[]{:S(2)}) collective-permute-start(bf16[1,2,16,768]{3,2,1,0:T(8,128)(2,1)S(1)} %first_keys.1.refs_3_), channel_id=1, source_target_pairs={{0,2},{1,3},{2,0},{3,1},{4,6},{5,7},{6,4},{7,5},{8,10},{9,11},{10,... | collective-permute-start | bytes 147464 | tf_op jit(solution)/shard_map/ppermute | solution.py:21
  7.7 15.3 %slice-start = ((s8[4718592]{0:T(1024)(128)(4,1)}), s8[4194304]{0:T(1024)(128)(4,1)S(1)}, s32[]{:S(2)}) async-start(s8[4718592]{0:T(1024)(128)(4,1)} %bitcast), calls=%async_computation | async-start | bytes 8388608
  10.6 3.5 %collective-permute-start.1 = (bf16[2,2,16,768]{3,2,1,0:T(8,128)(2,1)S(1)}, bf16[2,2,16,768]{3,2,1,0:T(8,128)(2,1)S(1)}, u32[]{:S(2)}, u32[]{:S(2)}) collective-permute-start(bf16[2,2,16,768]{3,2,1,0:T(8,128)(2,1)S(1)} %constant_dynamic-update-slice_fusion.refs_2_), channel_id=1, source_target_pairs={{0,4},{1,5},{2,6},{3,7},{4,0},{5,1},{6,2},{7,3},{8,12},{9,13},{10,... | collective-permute-start | bytes 294920 | tf_op jit(solution)/shard_map/ppermute | solution.py:21
  12.0 10.9 %slice-start.1 = ((s8[4718592]{0:T(1024)(128)(4,1)}), s8[524288]{0:T(1024)(128)(4,1)S(1)}, s32[]{:S(2)}) async-start(s8[4718592]{0:T(1024)(128)(4,1)} %bitcast), calls=%async_computation.1 | async-start | bytes 1048576
  12.0 10.9 %copy-start.2 = (bf16[768,768]{1,0:T(8,128)(2,1)S(1)}, bf16[768,768]{1,0:T(8,128)(2,1)}, u32[]{:S(2)}) copy-start(bf16[768,768]{1,0:T(8,128)(2,1)} %refs_2_.3) | copy-start | bytes 3538948
  13.6 3.0 %collective-permute-start.3 = (bf16[1,2,16,768]{3,2,1,0:T(8,128)(2,1)S(1)}, bf16[1,2,16,768]{3,2,1,0:T(8,128)(2,1)S(1)}, u32[]{:S(2)}, u32[]{:S(2)}) collective-permute-start(bf16[1,2,16,768]{3,2,1,0:T(8,128)(2,1)S(1)} %collective-permute-done), channel_id=1, source_target_pairs={{0,2},{1,3},{2,0},{3,1},{4,6},{5,7},{6,4},{7,5},{8,10},{9,11},{10,... | collective-permute-start | bytes 147464 | tf_op jit(solution)/shard_map/ppermute | solution.py:21
  13.9 9.1 %copy-start = (bf16[3072,768]{1,0:T(8,128)(2,1)S(1)}, bf16[3072,768]{1,0:T(8,128)(2,1)}, u32[]{:S(2)}) copy-start(bf16[3072,768]{1,0:T(8,128)(2,1)} %refs_4_.4) | copy-start | bytes 14155780
  14.2 3.5 %collective-permute-start.4 = (bf16[2,2,16,768]{3,2,1,0:T(8,128)(2,1)S(1)}, bf16[2,2,16,768]{3,2,1,0:T(8,128)(2,1)S(1)}, u32[]{:S(2)}, u32[]{:S(2)}) collective-permute-start(bf16[2,2,16,768]{3,2,1,0:T(8,128)(2,1)S(1)} %collective-permute-done.1), channel_id=1, source_target_pairs={{0,2},{1,3},{2,0},{3,1},{4,6},{5,7},{6,4},{7,5},{8,10},{9,11},{10,... | collective-permute-start | bytes 294920 | tf_op jit(solution)/shard_map/ppermute | solution.py:21
  17.7 5.3 %collective-permute-start.5 = (bf16[8,2,16,768]{3,2,1,0:T(8,128)(2,1)S(1)}, bf16[8,2,16,768]{3,2,1,0:T(8,128)(2,1)S(1)}, u32[]{:S(2)}, u32[]{:S(2)}) collective-permute-start(bf16[8,2,16,768]{3,2,1,0:T(8,128)(2,1)S(1)} %constant_dynamic-update-slice_fusion.2.keyval.refs_3_), channel_id=1, source_target_pairs={{0,1},{1,0},{2,3},{3,2},{4,5},{5,4},{6,7},{7,6},{8,9},{9,8},{10,11... | collective-permute-start | bytes 1179656 | tf_op jit(solution)/shard_map/ppermute | solution.py:21
  21.3 1.7 %copy-start.3 = (f32[768]{0:T(1024)S(1)}, f32[768]{0:T(1024)}, u32[]{:S(2)}) copy-start(f32[768]{0:T(1024)} %refs_3_.3) | copy-start | bytes 9220
  21.3 1.7 %copy-start.4 = (f32[768]{0:T(1024)S(1)}, f32[768]{0:T(1024)}, u32[]{:S(2)}) copy-start(f32[768]{0:T(1024)} %refs_3_.5) | copy-start | bytes 9220
  32.8 14.5 %collective-permute-start.6 = (bf16[1,2,16,768]{3,2,1,0:T(8,128)(2,1)S(1)}, bf16[1,2,16,768]{3,2,1,0:T(8,128)(2,1)S(1)}, u32[]{:S(2)}, u32[]{:S(2)}) collective-permute-start(bf16[1,2,16,768]{3,2,1,0:T(8,128)(2,1)S(1)} %get-tuple-element.53.refs_8_), channel_id=1, source_target_pairs={{0,8},{1,3},{2,10},{3,1},{4,12},{5,7},{6,14},{7,5},{8,0},{9,11},{1... | collective-permute-start | bytes 147464 | tf_op jit(solution)/shard_map/ppermute | solution.py:834
  33.3 13.3 %copy-start.1 = (bf16[768,768]{1,0:T(8,128)(2,1)S(1)}, bf16[768,768]{1,0:T(8,128)(2,1)}, u32[]{:S(2)}) copy-start(bf16[768,768]{1,0:T(8,128)(2,1)} %refs_4_.5) | copy-start | bytes 3538948
  47.3 5.8 %collective-permute-start.7 = (bf16[2,2,16,768]{3,2,1,0:T(8,128)(2,1)S(1)}, bf16[2,2,16,768]{3,2,1,0:T(8,128)(2,1)S(1)}, u32[]{:S(2)}, u32[]{:S(2)}) collective-permute-start(bf16[2,2,16,768]{3,2,1,0:T(8,128)(2,1)S(1)} %constant_dynamic-update-slice_fusion.7.refs_5_), channel_id=1, source_target_pairs={{0,4},{1,9},{2,6},{3,11},{4,0},{5,13},{6,2},{7,15},{8,12},{9,1},{1... | collective-permute-start | bytes 294920 | tf_op jit(solution)/shard_map/ppermute | solution.py:834
  53.1 6.6 %collective-permute-start.8 = (bf16[4,2,16,768]{3,2,1,0:T(8,128)(2,1)S(1)}, bf16[4,2,16,768]{3,2,1,0:T(8,128)(2,1)S(1)}, u32[]{:S(2)}, u32[]{:S(2)}) collective-permute-start(bf16[4,2,16,768]{3,2,1,0:T(8,128)(2,1)S(1)} %constant_dynamic-update-slice_fusion.9.refs_5_), channel_id=1, source_target_pairs={{0,2},{1,5},{2,0},{3,7},{4,6},{5,1},{6,4},{7,3},{8,10},{9,13},{10,... | collective-permute-start | bytes 589832 | tf_op jit(solution)/shard_map/ppermute | solution.py:834
  59.7 2.6 %collective-permute-start.9 = (bf16[8,2,16,768]{3,2,1,0:T(8,128)(2,1)S(1)}, bf16[8,2,16,768]{3,2,1,0:T(8,128)(2,1)S(1)}, u32[]{:S(2)}, u32[]{:S(2)}) collective-permute-start(bf16[8,2,16,768]{3,2,1,0:T(8,128)(2,1)S(1)} %constant_dynamic-update-slice_fusion.11.refs_5_), channel_id=1, source_target_pairs={{0,1},{1,0},{2,3},{3,2},{4,5},{5,4},{6,7},{7,6},{8,9},{9,8},{10,11... | collective-permute-start | bytes 1179656 | tf_op jit(solution)/shard_map/ppermute | solution.py:21

commit v3 on v2

--- a/solution.py
+++ b/solution.py
@@ -251,22 +251,27 @@
 def first_keys_kernel(
     offsets, tokens, gain, key_weight, value_weight, keyval, rows, wide, picks, scale, sems, *, stride
 ):
+    spans = pieces(tokens.shape[0], tokens.shape[0] // 4)
     copies = [
         bring(offsets, picks, sems.at[0]),
-        bring(tokens, rows, sems.at[1]),
-        bring(gain, scale, sems.at[2]),
-        bring(key_weight, wide.at[0], sems.at[3]),
-        bring(value_weight, wide.at[1], sems.at[4]),
+        bring(gain, scale, sems.at[1]),
+        *[bring(tokens.at[x], rows.at[x], sems.at[4 + i]) for i, x in enumerate(spans)],
+        bring(key_weight, wide.at[0], sems.at[2]),
+        bring(value_weight, wide.at[1], sems.at[3]),
     ]
     heads = offsets.shape[0]
     copies[0].wait()
     chooser = pick_matrix(picks, heads, rows.shape[0] // stride, stride)
     copies[1].wait()
-    copies[2].wait()
-    chosen = norm_rows(dot(chooser, rows[...]), scale[...])
+    chosen = None
+    for copy, span in zip(copies[2:-2], spans):
+        copy.wait()
+        part = dot(chooser[:, span], rows[span, :])
+        chosen = part if chosen is None else chosen + part
+    chosen = norm_rows(chosen, scale[...])
 
     def weight(slot):
-        copies[slot + 3].wait()
+        copies[slot - 2].wait()
         return wide[slot]
 
     project_keys(
@@ -323,15 +328,21 @@
     return head_size ** (-0.5) * LOG2E
 
 
+def project_rows(normed, span, weight, out, peak):
+    query = dot(normed[span, :], weight[...])
+    out[...] = query.astype(BF16)
+    for part in pieces(query.shape[0], 64):
+        square = query[part] * query[part]
+        peak = square if peak is None else jnp.maximum(peak, square)
+    return peak
+
+
 def project_query(normed, weight, outs, heads, peaks):
     peak = None
     for out, row in outs:
         for span in pieces(out.shape[0], 512 if out.shape[0] % 512 == 0 else 256):
-            query = dot(normed[row + span.start : row + span.stop, :], weight[...])
-            out[span, :] = query.astype(BF16)
-            for part in pieces(query.shape[0], 64):
-                square = query[part] * query[part]
-                peak = square if peak is None else jnp.maximum(peak, square)
+            place = slice(row + span.start, row + span.stop)
+            peak = project_rows(normed, place, weight, out.at[span], peak)
     peaks[...] = summed_peaks(peak.astype(BF16), heads)
 
 
@@ -602,7 +613,7 @@
 
 def add_heads(tokens, first_row, mixed, out_weight, gain, first, normed):
     before = None
-    for span in pieces(mixed.shape[0], 256):
+    for span in pieces(mixed.shape[0], 384):
         total = dot(mixed[span, :], out_weight[...])
         rows = tokens[first_row + span.start : first_row + span.stop, :]
         first[span, :] = (rows.astype(F32) + total).astype(BF16)
@@ -740,10 +751,20 @@
     del sems
     start = picked.shape[0]
     query[:start, :] = picked[...]
-    norm_into(normed, 0, rows, gain[...], rows.shape[0])
-    out = query.at[pl.ds(start, rows.shape[0])]
-    project_query(normed, weight, [(out, 0)], heads, peaks)
-    peaks[...] = jnp.maximum(peaks[...], picked_peaks[...])
+    spans = pieces(rows.shape[0], rows.shape[0] // 2)
+
+    def norm_part(i):
+        span = spans[i]
+        norm_into(normed, span.start, rows.at[span], gain[...], span.stop - span.start)
+
+    norm_part(0)
+    peak = None
+    for i, span in enumerate(spans):
+        out = query.at[pl.ds(start + span.start, span.stop - span.start)]
+        peak = project_rows(normed, span, weight, out, peak)
+        if i + 1 < len(spans):
+            norm_part(i + 1)
+    peaks[...] = jnp.maximum(summed_peaks(peak.astype(BF16), heads), picked_peaks[...])
 
 
 def second_kernel(*refs, heads, parts):
@@ -899,7 +920,7 @@
         (segment_offset, tokens, attn_gain, key_first, segment_value),
         [near(count, width), near(2, width, width)] + small_work,
         far=(0, 1, 2, 3, 4),
-        copies=5,
+        copies=8,
         flops=2 * heads * groups * width * (count + 2 * width),
         name="first_keys",
     )

time: 83.4 us -> 83.3 us (level)
  no operation moved by 1% of the time
where the time goes in v3:
time: 83.3 us; the launch traced here: 83.2 us
  Pallas kernels  64.9 us (78%)
  starting transfers between devices  15 us (18%)
  waiting for transfers between devices  2.69 us (3%)
    pallas_call x11, Pallas kernels, local_call(): pl.pallas_call(kernel, out_shape=outs, in_specs=specs, out_specs=[pl.Bloc...  64.9 us
    ppermute x7, starting transfers between devices, swapped(): lax.ppermute(x, axis, [(i, i ^ 1 << apart) for i in range(lax.axis_size(a...  11.7 us
    ppermute x3, starting transfers between devices, exchange(): partner = lax.ppermute(keyval, 'seq', pairs)  3.3 us
    ppermute x7, waiting for transfers between devices, swapped(): lax.ppermute(x, axis, [(i, i ^ 1 << apart) for i in range(lax.axis_size(a...  2.68 us
  transfers between devices with their start and end apart: 10, of which 3 were waited for; matrix products, arithmetic and copies ran while one was open for 0% of the time, Pallas kernels for 38%

profile of v3, /device:TPU:1, one launch (start us, length us, event | category | flops | bytes accessed | tf_op | source)
XLA Modules:
  0.0 83.2 jit_solution(18054908992896635095)
XLA Ops:
  0.0 3.1 %first_keys.1.refs_3_ = bf16[1,2,16,768]{3,2,1,0:T(8,128)(2,1)S(1)} custom-call(s32[16]{0:T(128)} %offsets.1, bf16[1024,768]{1,0:T(8,128)(2,1)} %refs_1_.3, f32[768]{0:T(1024)} %refs_2_.2, bf16[768,768]{1,0:T(8,128)(2,1)} %key_weight.2, bf16[768,768]{1,0:T(8,128)(2,1)} %value_weight.2), custom_call_target="tpu_custom_call" | custom-call | flops 1006632960 | bytes 3935296 | tf_op jit(solution)/shard_map/first_keys/pallas_call | solution.py:830
  3.1 3.2 %collective-permute-start = (bf16[1,2,16,768]{3,2,1,0:T(8,128)(2,1)S(1)}, bf16[1,2,16,768]{3,2,1,0:T(8,128)(2,1)S(1)}, u32[]{:S(2)}, u32[]{:S(2)}) collective-permute-start(bf16[1,2,16,768]{3,2,1,0:T(8,128)(2,1)S(1)} %first_keys.1.refs_3_), channel_id=1, source_target_pairs={{0,8},{1,9},{2,10},{3,11},{4,12},{5,13},{6,14},{7,15},{8,0},{9,1},... | collective-permute-start | bytes 147464 | tf_op jit(solution)/shard_map/ppermute | solution.py:21
  6.3 1.2 %collective-permute-start.2 = (bf16[1,2,16,768]{3,2,1,0:T(8,128)(2,1)S(1)}, bf16[1,2,16,768]{3,2,1,0:T(8,128)(2,1)S(1)}, u32[]{:S(2)}, u32[]{:S(2)}) collective-permute-start(bf16[1,2,16,768]{3,2,1,0:T(8,128)(2,1)S(1)} %first_keys.1.refs_3_), channel_id=1, source_target_pairs={{0,2},{1,3},{2,0},{3,1},{4,6},{5,7},{6,4},{7,5},{8,10},{9,11},{10,... | collective-permute-start | bytes 147464 | tf_op jit(solution)/shard_map/ppermute | solution.py:21
  7.5 2.9 %order.1 = (bf16[1024,768]{1,0:T(8,128)(2,1)S(1)}, bf16[1024,768]{1,0:T(8,128)(2,1)S(1)}, bf16[256,256]{1,0:T(8,128)(2,1)S(1)}, bf16[256,256]{1,0:T(8,128)(2,1)S(1)}, bf16[1,2,16,768]{3,2,1,0:T(8,128)(2,1)S(1)}) custom-call(s32[16]{0:T(128)} %refs_0_.1, bf16[1024,768]{1,0:T(8,128)(2,1)} %refs_1_.3, f32[768]{0:T(1024)} %refs_2_.2, ...), custom_call_target="tpu_custom_call" | custom-call | flops 402653184 | bytes 1576000 | tf_op jit(solution)/shard_map/order/pallas_call | solution.py:830
  10.5 0.0 collective-permute-done
  10.5 1.4 %collective-permute-start.1 = (bf16[2,2,16,768]{3,2,1,0:T(8,128)(2,1)S(1)}, bf16[2,2,16,768]{3,2,1,0:T(8,128)(2,1)S(1)}, u32[]{:S(2)}, u32[]{:S(2)}) collective-permute-start(bf16[2,2,16,768]{3,2,1,0:T(8,128)(2,1)S(1)} %constant_dynamic-update-slice_fusion.refs_2_), channel_id=1, source_target_pairs={{0,4},{1,5},{2,6},{3,7},{4,0},{5,1},{6,2},{7,3},{8,12},{9,13},{10,... | collective-permute-start | bytes 294920 | tf_op jit(solution)/shard_map/ppermute | solution.py:21
  11.8 0.0 copy-done.5
  11.9 1.6 %first_query.1 = (bf16[256,768]{1,0:T(8,128)(2,1)S(1)}, bf16[768,768]{1,0:T(8,128)(2,1)S(1)}, f32[1,128]{1,0:T(1,128)S(1)}, bf16[2,2,16,768]{3,2,1,0:T(8,128)(2,1)S(1)}) custom-call(bf16[1024,768]{1,0:T(8,128)(2,1)S(1)} %get-tuple-element.40.refs_0_, bf16[768,768]{1,0:T(8,128)(2,1)S(1)} %copy-done.5, ...), custom_call_target="tpu_custom_call" | custom-call | flops 1207959552 | tf_op jit(solution)/shard_map/first_query/pallas_call | solution.py:830
  13.4 0.3 collective-permute-start.3
  13.7 0.3 collective-permute-done.1
  14.0 1.0 %collective-permute-start.4 = (bf16[2,2,16,768]{3,2,1,0:T(8,128)(2,1)S(1)}, bf16[2,2,16,768]{3,2,1,0:T(8,128)(2,1)S(1)}, u32[]{:S(2)}, u32[]{:S(2)}) collective-permute-start(bf16[2,2,16,768]{3,2,1,0:T(8,128)(2,1)S(1)} %collective-permute-done.1), channel_id=1, source_target_pairs={{0,2},{1,3},{2,0},{3,1},{4,6},{5,7},{6,4},{7,5},{8,10},{9,11},{10,... | collective-permute-start | bytes 294920 | tf_op jit(solution)/shard_map/ppermute | solution.py:21
  15.1 0.0 collective-permute-done.2
  15.1 1.4 %collective-permute-done.3 = bf16[1,2,16,768]{3,2,1,0:T(8,128)(2,1)S(1)} collective-permute-done((bf16[1,2,16,768]{3,2,1,0:T(8,128)(2,1)S(1)}, bf16[1,2,16,768]{3,2,1,0:T(8,128)(2,1)S(1)}, u32[]{:S(2)}, u32[]{:S(2)}) %collective-permute-start.3) | collective-permute-done | bytes 49184 | tf_op jit(solution)/shard_map/ppermute | solution.py:21
  16.4 1.0 %collective-permute-done.4 = bf16[2,2,16,768]{3,2,1,0:T(8,128)(2,1)S(1)} collective-permute-done((bf16[2,2,16,768]{3,2,1,0:T(8,128)(2,1)S(1)}, bf16[2,2,16,768]{3,2,1,0:T(8,128)(2,1)S(1)}, u32[]{:S(2)}, u32[]{:S(2)}) %collective-permute-start.4) | collective-permute-done | bytes 98336 | tf_op jit(solution)/shard_map/ppermute | solution.py:21
  17.5 3.6 %collective-permute-start.5 = (bf16[8,2,16,768]{3,2,1,0:T(8,128)(2,1)S(1)}, bf16[8,2,16,768]{3,2,1,0:T(8,128)(2,1)S(1)}, u32[]{:S(2)}, u32[]{:S(2)}) collective-permute-start(bf16[8,2,16,768]{3,2,1,0:T(8,128)(2,1)S(1)} %constant_dynamic-update-slice_fusion.2.keyval.refs_3_), channel_id=1, source_target_pairs={{0,1},{1,0},{2,3},{3,2},{4,5},{5,4},{6,7},{7,6},{8,9},{9,8},{10,11... | collective-permute-start | bytes 1179656 | tf_op jit(solution)/shard_map/ppermute | solution.py:21
  21.1 1.7 %near_weights.1 = (bf16[16,256,128]{2,1,0:T(8,128)(2,1)S(1)}, bf16[16,768,128]{2,1,0:T(8,128)(2,1)S(1)}, bf16[768,128]{1,0:T(8,128)(2,1)S(1)}, f32[1,128]{1,0:T(1,128)S(1)}) custom-call(bf16[256,768]{1,0:T(8,128)(2,1)S(1)} %get-tuple-element.42.picked.query, bf16[768,768]{1,0:T(8,128)(2,1)S(1)} %get-tuple-element.44.rest.refs_0_, ...), custom_call_target="tpu_custom_call" | custom-call | flops 1073741824 | tf_op jit(solution)/shard_map/near_weights/pallas_call | solution.py:830
  22.8 0.0 collective-permute-done.5.keyval_far.refs_4_
  22.8 9.8 %layer_of_picked.1 = (bf16[256,768]{1,0:T(8,128)(2,1)S(1)}, bf16[256,768]{1,0:T(8,128)(2,1)S(1)}, bf16[1,2,16,768]{3,2,1,0:T(8,128)(2,1)S(1)}, bf16[768,128]{1,0:T(8,128)(2,1)S(1)}, f32[1,128]{1,0:T(1,128)S(1)}) custom-call(bf16[256,256]{1,0:T(8,128)(2,1)S(1)} %get-tuple-element.38.chooser, bf16[1024,768]{1,0:T(8,128)(2,1)S(1)} %get-tuple-element.39.tokens.refs_0_, ...), custom_call_target="tpu_custom_call" | custom-call | flops 3791650816 | bytes 2359296 | tf_op jit(solution)/shard_map/layer_of_picked/pallas_call | solution.py:830
  32.6 0.5 collective-permute-start.6
  33.1 13.3 %rest_attention.1 = (bf16[768,768]{1,0:T(8,128)(2,1)S(1)}, bf16[1,2,16,768]{3,2,1,0:T(8,128)(2,1)S(1)}) custom-call(bf16[768,768]{1,0:T(8,128)(2,1)S(1)} %get-tuple-element.44.rest.refs_0_, f32[1,128]{1,0:T(1,128)S(1)} %get-tuple-element.43.query_peaks.refs_1_, bf16[16,768,128]{2,1,0:T(8,128)(2,1)S(1)} %get-tuple-element.50.refs_2_, ...), custom_call_target="tpu_custom_call" | custom-call | flops 3221225472 | tf_op jit(solution)/shard_map/rest_attention/pallas_call | solution.py:830
  46.4 0.7 picked_query.1
  47.1 0.0 collective-permute-done.6
  47.1 1.1 %collective-permute-start.7 = (bf16[2,2,16,768]{3,2,1,0:T(8,128)(2,1)S(1)}, bf16[2,2,16,768]{3,2,1,0:T(8,128)(2,1)S(1)}, u32[]{:S(2)}, u32[]{:S(2)}) collective-permute-start(bf16[2,2,16,768]{3,2,1,0:T(8,128)(2,1)S(1)} %constant_dynamic-update-slice_fusion.7.refs_5_), channel_id=1, source_target_pairs={{0,4},{1,9},{2,6},{3,11},{4,0},{5,13},{6,2},{7,15},{8,12},{9,1},{1... | collective-permute-start | bytes 294920 | tf_op jit(solution)/shard_map/ppermute | solution.py:855
  48.2 4.7 %rest_up.1 = (bf16[768,768]{1,0:T(8,128)(2,1)S(1)}, bf16[768,768]{1,0:T(8,128)(2,1)S(1)}, bf16[768,2304]{1,0:T(8,128)(2,1)S(1)}, bf16[2,2,16,768]{3,2,1,0:T(8,128)(2,1)S(1)}) custom-call(bf16[1024,768]{1,0:T(8,128)(2,1)S(1)} %get-tuple-element.39.tokens.refs_0_, bf16[768,768]{1,0:T(8,128)(2,1)S(1)} %get-tuple-element.54.refs_1_, ...), custom_call_target="tpu_custom_call" | custom-call | flops 3623878656 | tf_op jit(solution)/shard_map/rest_up/pallas_call | solution.py:830
  53.0 0.0 collective-permute-done.7
  53.0 1.7 %collective-permute-start.8 = (bf16[4,2,16,768]{3,2,1,0:T(8,128)(2,1)S(1)}, bf16[4,2,16,768]{3,2,1,0:T(8,128)(2,1)S(1)}, u32[]{:S(2)}, u32[]{:S(2)}) collective-permute-start(bf16[4,2,16,768]{3,2,1,0:T(8,128)(2,1)S(1)} %constant_dynamic-update-slice_fusion.9.refs_5_), channel_id=1, source_target_pairs={{0,2},{1,5},{2,0},{3,7},{4,6},{5,1},{6,4},{7,3},{8,10},{9,13},{10,... | collective-permute-start | bytes 589832 | tf_op jit(solution)/shard_map/ppermute | solution.py:855
  54.7 4.8 %rest_down.1 = (bf16[768,768]{1,0:T(8,128)(2,1)S(1)}, bf16[4,2,16,768]{3,2,1,0:T(8,128)(2,1)S(1)}) custom-call(bf16[768,768]{1,0:T(8,128)(2,1)S(1)} %get-tuple-element.58.refs_0_, bf16[768,768]{1,0:T(8,128)(2,1)S(1)} %get-tuple-element.59.refs_1_, bf16[768,2304]{1,0:T(8,128)(2,1)S(1)} %get-tuple-element.60.refs_2_, bf16[768,3072]{1,0:T(8,128)(2,1)S(1)} %bitcast.1, ...), custom_call_target="tpu_custom_call" | custom-call | flops 4529848320 | tf_op jit(solution)/shard_map/rest_down/pallas_call | solution.py:830
  59.6 0.0 collective-permute-done.8
  59.6 0.9 %collective-permute-start.9 = (bf16[8,2,16,768]{3,2,1,0:T(8,128)(2,1)S(1)}, bf16[8,2,16,768]{3,2,1,0:T(8,128)(2,1)S(1)}, u32[]{:S(2)}, u32[]{:S(2)}) collective-permute-start(bf16[8,2,16,768]{3,2,1,0:T(8,128)(2,1)S(1)} %constant_dynamic-update-slice_fusion.11.refs_5_), channel_id=1, source_target_pairs={{0,1},{1,0},{2,3},{3,2},{4,5},{5,4},{6,7},{7,6},{8,9},{9,8},{10,11... | collective-permute-start | bytes 1179656 | tf_op jit(solution)/shard_map/ppermute | solution.py:21
  60.6 1.7 %rest_query.1 = (bf16[1024,768]{1,0:T(8,128)(2,1)S(1)}, f32[1,128]{1,0:T(1,128)S(1)}, bf16[8,2,16,768]{3,2,1,0:T(8,128)(2,1)S(1)}) custom-call(bf16[256,768]{1,0:T(8,128)(2,1)S(1)} %get-tuple-element.63.refs_0_, f32[1,128]{1,0:T(1,128)S(1)} %get-tuple-element.64.refs_1_, bf16[768,768]{1,0:T(8,128)(2,1)S(1)} %get-tuple-element.62.refs_2_, f32[768]{0:T(1024)S(1)} %copy-done.4, ...), custom_call_target="tpu_custom_call" | custom-call | flops 905969664 | tf_op jit(solution)/shard_map/rest_query/pallas_call | solution.py:830
  62.3 0.0 collective-permute-done.9.refs_6_
  62.3 20.7 %second_attention.1 = bf16[1024,768]{1,0:T(8,128)(2,1)} custom-call(bf16[256,256]{1,0:T(8,128)(2,1)S(1)} %get-tuple-element.37.refs_0_, bf16[256,768]{1,0:T(8,128)(2,1)S(1)} %get-tuple-element.49.refs_1_, bf16[768,768]{1,0:T(8,128)(2,1)S(1)} %get-tuple-element.62.refs_2_, bf16[1024,768]{1,0:T(8,128)(2,1)S(1)} %get-tuple-element.66.refs_3_, ...), custom_call_target="tpu_custom_call" | custom-call | flops 5502926848 | bytes 1179648 | tf_op jit(solution)/shard_map/second_attention/pallas_call | solution.py:830
  (29 shorter events, 0.1 us)
Async XLA Ops:
  0.0 11.9 %copy-start.5 = (bf16[768,768]{1,0:T(8,128)(2,1)S(1)}, bf16[768,768]{1,0:T(8,128)(2,1)}, u32[]{:S(2)}) copy-start(bf16[768,768]{1,0:T(8,128)(2,1)} %refs_1_.4) | copy-start | bytes 3538948
  3.1 7.4 %collective-permute-start = (bf16[1,2,16,768]{3,2,1,0:T(8,128)(2,1)S(1)}, bf16[1,2,16,768]{3,2,1,0:T(8,128)(2,1)S(1)}, u32[]{:S(2)}, u32[]{:S(2)}) collective-permute-start(bf16[1,2,16,768]{3,2,1,0:T(8,128)(2,1)S(1)} %first_keys.1.refs_3_), channel_id=1, source_target_pairs={{0,8},{1,9},{2,10},{3,11},{4,12},{5,13},{6,14},{7,15},{8,0},{9,1},... | collective-permute-start | bytes 147464 | tf_op jit(solution)/shard_map/ppermute | solution.py:21
  6.3 8.8 %collective-permute-start.2 = (bf16[1,2,16,768]{3,2,1,0:T(8,128)(2,1)S(1)}, bf16[1,2,16,768]{3,2,1,0:T(8,128)(2,1)S(1)}, u32[]{:S(2)}, u32[]{:S(2)}) collective-permute-start(bf16[1,2,16,768]{3,2,1,0:T(8,128)(2,1)S(1)} %first_keys.1.refs_3_), channel_id=1, source_target_pairs={{0,2},{1,3},{2,0},{3,1},{4,6},{5,7},{6,4},{7,5},{8,10},{9,11},{10,... | collective-permute-start | bytes 147464 | tf_op jit(solution)/shard_map/ppermute | solution.py:21
  7.5 15.3 %slice-start = ((s8[4718592]{0:T(1024)(128)(4,1)}), s8[4194304]{0:T(1024)(128)(4,1)S(1)}, s32[]{:S(2)}) async-start(s8[4718592]{0:T(1024)(128)(4,1)} %bitcast), calls=%async_computation | async-start | bytes 8388608
  10.5 3.5 %collective-permute-start.1 = (bf16[2,2,16,768]{3,2,1,0:T(8,128)(2,1)S(1)}, bf16[2,2,16,768]{3,2,1,0:T(8,128)(2,1)S(1)}, u32[]{:S(2)}, u32[]{:S(2)}) collective-permute-start(bf16[2,2,16,768]{3,2,1,0:T(8,128)(2,1)S(1)} %constant_dynamic-update-slice_fusion.refs_2_), channel_id=1, source_target_pairs={{0,4},{1,5},{2,6},{3,7},{4,0},{5,1},{6,2},{7,3},{8,12},{9,13},{10,... | collective-permute-start | bytes 294920 | tf_op jit(solution)/shard_map/ppermute | solution.py:21
  11.9 10.9 %slice-start.1 = ((s8[4718592]{0:T(1024)(128)(4,1)}), s8[524288]{0:T(1024)(128)(4,1)S(1)}, s32[]{:S(2)}) async-start(s8[4718592]{0:T(1024)(128)(4,1)} %bitcast), calls=%async_computation.1 | async-start | bytes 1048576
  11.9 10.9 %copy-start.2 = (bf16[768,768]{1,0:T(8,128)(2,1)S(1)}, bf16[768,768]{1,0:T(8,128)(2,1)}, u32[]{:S(2)}) copy-start(bf16[768,768]{1,0:T(8,128)(2,1)} %refs_2_.3) | copy-start | bytes 3538948
  13.4 3.0 %collective-permute-start.3 = (bf16[1,2,16,768]{3,2,1,0:T(8,128)(2,1)S(1)}, bf16[1,2,16,768]{3,2,1,0:T(8,128)(2,1)S(1)}, u32[]{:S(2)}, u32[]{:S(2)}) collective-permute-start(bf16[1,2,16,768]{3,2,1,0:T(8,128)(2,1)S(1)} %collective-permute-done), channel_id=1, source_target_pairs={{0,2},{1,3},{2,0},{3,1},{4,6},{5,7},{6,4},{7,5},{8,10},{9,11},{10,... | collective-permute-start | bytes 147464 | tf_op jit(solution)/shard_map/ppermute | solution.py:21
  13.7 9.1 %copy-start = (bf16[3072,768]{1,0:T(8,128)(2,1)S(1)}, bf16[3072,768]{1,0:T(8,128)(2,1)}, u32[]{:S(2)}) copy-start(bf16[3072,768]{1,0:T(8,128)(2,1)} %refs_4_.4) | copy-start | bytes 14155780
  14.0 3.5 %collective-permute-start.4 = (bf16[2,2,16,768]{3,2,1,0:T(8,128)(2,1)S(1)}, bf16[2,2,16,768]{3,2,1,0:T(8,128)(2,1)S(1)}, u32[]{:S(2)}, u32[]{:S(2)}) collective-permute-start(bf16[2,2,16,768]{3,2,1,0:T(8,128)(2,1)S(1)} %collective-permute-done.1), channel_id=1, source_target_pairs={{0,2},{1,3},{2,0},{3,1},{4,6},{5,7},{6,4},{7,5},{8,10},{9,11},{10,... | collective-permute-start | bytes 294920 | tf_op jit(solution)/shard_map/ppermute | solution.py:21
  17.5 5.3 %collective-permute-start.5 = (bf16[8,2,16,768]{3,2,1,0:T(8,128)(2,1)S(1)}, bf16[8,2,16,768]{3,2,1,0:T(8,128)(2,1)S(1)}, u32[]{:S(2)}, u32[]{:S(2)}) collective-permute-start(bf16[8,2,16,768]{3,2,1,0:T(8,128)(2,1)S(1)} %constant_dynamic-update-slice_fusion.2.keyval.refs_3_), channel_id=1, source_target_pairs={{0,1},{1,0},{2,3},{3,2},{4,5},{5,4},{6,7},{7,6},{8,9},{9,8},{10,11... | collective-permute-start | bytes 1179656 | tf_op jit(solution)/shard_map/ppermute | solution.py:21
  21.1 1.7 %copy-start.3 = (f32[768]{0:T(1024)S(1)}, f32[768]{0:T(1024)}, u32[]{:S(2)}) copy-start(f32[768]{0:T(1024)} %refs_3_.3) | copy-start | bytes 9220
  21.1 1.7 %copy-start.4 = (f32[768]{0:T(1024)S(1)}, f32[768]{0:T(1024)}, u32[]{:S(2)}) copy-start(f32[768]{0:T(1024)} %refs_3_.5) | copy-start | bytes 9220
  32.6 14.5 %collective-permute-start.6 = (bf16[1,2,16,768]{3,2,1,0:T(8,128)(2,1)S(1)}, bf16[1,2,16,768]{3,2,1,0:T(8,128)(2,1)S(1)}, u32[]{:S(2)}, u32[]{:S(2)}) collective-permute-start(bf16[1,2,16,768]{3,2,1,0:T(8,128)(2,1)S(1)} %get-tuple-element.53.refs_8_), channel_id=1, source_target_pairs={{0,8},{1,3},{2,10},{3,1},{4,12},{5,7},{6,14},{7,5},{8,0},{9,11},{1... | collective-permute-start | bytes 147464 | tf_op jit(solution)/shard_map/ppermute | solution.py:855
  33.1 13.3 %copy-start.1 = (bf16[768,768]{1,0:T(8,128)(2,1)S(1)}, bf16[768,768]{1,0:T(8,128)(2,1)}, u32[]{:S(2)}) copy-start(bf16[768,768]{1,0:T(8,128)(2,1)} %refs_4_.5) | copy-start | bytes 3538948
  47.1 5.9 %collective-permute-start.7 = (bf16[2,2,16,768]{3,2,1,0:T(8,128)(2,1)S(1)}, bf16[2,2,16,768]{3,2,1,0:T(8,128)(2,1)S(1)}, u32[]{:S(2)}, u32[]{:S(2)}) collective-permute-start(bf16[2,2,16,768]{3,2,1,0:T(8,128)(2,1)S(1)} %constant_dynamic-update-slice_fusion.7.refs_5_), channel_id=1, source_target_pairs={{0,4},{1,9},{2,6},{3,11},{4,0},{5,13},{6,2},{7,15},{8,12},{9,1},{1... | collective-permute-start | bytes 294920 | tf_op jit(solution)/shard_map/ppermute | solution.py:855
  53.0 6.6 %collective-permute-start.8 = (bf16[4,2,16,768]{3,2,1,0:T(8,128)(2,1)S(1)}, bf16[4,2,16,768]{3,2,1,0:T(8,128)(2,1)S(1)}, u32[]{:S(2)}, u32[]{:S(2)}) collective-permute-start(bf16[4,2,16,768]{3,2,1,0:T(8,128)(2,1)S(1)} %constant_dynamic-update-slice_fusion.9.refs_5_), channel_id=1, source_target_pairs={{0,2},{1,5},{2,0},{3,7},{4,6},{5,1},{6,4},{7,3},{8,10},{9,13},{10,... | collective-permute-start | bytes 589832 | tf_op jit(solution)/shard_map/ppermute | solution.py:855
  59.6 2.7 %collective-permute-start.9 = (bf16[8,2,16,768]{3,2,1,0:T(8,128)(2,1)S(1)}, bf16[8,2,16,768]{3,2,1,0:T(8,128)(2,1)S(1)}, u32[]{:S(2)}, u32[]{:S(2)}) collective-permute-start(bf16[8,2,16,768]{3,2,1,0:T(8,128)(2,1)S(1)} %constant_dynamic-update-slice_fusion.11.refs_5_), channel_id=1, source_target_pairs={{0,1},{1,0},{2,3},{3,2},{4,5},{5,4},{6,7},{7,6},{8,9},{9,8},{10,11... | collective-permute-start | bytes 1179656 | tf_op jit(solution)/shard_map/ppermute | solution.py:21
